TPU v7x, 256 devices: a whole 4x4x8 slice. The times are simulated.
256 devices in a mesh: row: 64 (over x, z, core), col: 4 (over y).
Axes of the slice: x: 4, y: 4, z: 8, core: 2. Of those that a mesh axis runs over, the one named last changes fastest.
Arguments:
- matrix: float32 [1, 64, 16, 4, 36864], P(None, 'row', None, 'col'), may hold values from -12 to 400, as said below
- panel_index: int32 [1], replicated, may hold values from 0 to 61
Outputs:
- updated: float32 [1, 64, 16, 4, 36864], P(None, 'row', None, 'col')
Inputs may be any that keep to these rules, and one draw needn't show every extreme that they name: `matrix`: symmetric; each diagonal tile that the 3 steps factor is positive definite at the time it is factored.
All inputs are finite; a program needn't handle non-finite values.
Results may differ from a plain program's by a relative error of at most 0.0001.
Values sent between devices are 32-bit elements; how exact they have to be, the bound alone decides.
A program may use at most 128 MiB of HBM per device.

v0:
```python
import jax
import jax.numpy as jnp
from jax import lax
from jax.sharding import PartitionSpec as P

B = 192
ITERS = 3


def from_root(array, axis, root):
    mine = lax.axis_index(axis) == root
    return lax.psum(jnp.where(mine, array, jnp.zeros_like(array)), axis)


def body(matrix, panel_index):
    row_count = matrix.shape[0]
    col_count = matrix.shape[2]
    tile = B
    n_row = lax.axis_size("row")
    n_col = lax.axis_size("col")
    my_row = lax.axis_index("row")
    my_col = lax.axis_index("col")
    local = matrix.reshape(row_count, col_count, tile, tile)
    row_tiles = jnp.arange(row_count, dtype=jnp.int32) * n_row + my_row
    col_tiles = jnp.arange(col_count, dtype=jnp.int32) * n_col + my_col
    identity = jnp.eye(tile, dtype=jnp.float32)
    for step in range(ITERS):
        panel = panel_index[0] + step
        owner_row = panel % n_row
        owner_col = panel % n_col
        col_slot = panel // n_col
        row_slot = panel // n_row
        column = lax.dynamic_index_in_dim(local, col_slot, 1, keepdims=False)
        candidate = lax.dynamic_index_in_dim(column, row_slot, 0, keepdims=False)
        is_owner = jnp.logical_and(my_row == owner_row, my_col == owner_col)
        candidate = jnp.where(is_owner, candidate, identity)
        flat_column = column.reshape(row_count * tile, tile)
        block = from_root(candidate, "row", owner_row)
        factor = jnp.linalg.cholesky(block)
        solved = lax.linalg.triangular_solve(
            factor, flat_column, left_side=False, lower=True, transpose_a=True
        )
        panel_tiles = from_root(solved.reshape(row_count, tile, tile), "col", owner_col)
        every = lax.all_gather(panel_tiles[:, None], "row", axis=1, tiled=True)
        grouped = every.reshape(col_count, n_col, tile, tile)
        partner = lax.dynamic_index_in_dim(grouped, my_col, 1, keepdims=False)
        row_below = (row_tiles > panel)[:, None, None]
        row_live = jnp.where(row_below, panel_tiles, jnp.zeros_like(panel_tiles))
        col_live = jnp.where((col_tiles > panel)[:, None, None], partner, jnp.zeros_like(partner))
        update = jnp.einsum(
            "rab,cdb->rcad",
            row_live,
            col_live,
            precision=lax.Precision.HIGHEST,
            preferred_element_type=jnp.float32,
        )
        local = local - update
        previous = lax.dynamic_index_in_dim(local, col_slot, 1, keepdims=False)
        fresh = jnp.where(
            row_below,
            panel_tiles,
            jnp.where((row_tiles == panel)[:, None, None], factor[None], previous),
        )
        fresh = jnp.where(my_col == owner_col, fresh, previous)
        local = lax.dynamic_update_index_in_dim(local, fresh, col_slot, 1)
    return local.reshape(matrix.shape)


def solution(mesh):
    in_specs = (P(None, "row", None, "col", None), P())
    out_specs = P(None, "row", None, "col", None)
    return jax.shard_map(body, mesh=mesh, in_specs=in_specs, out_specs=out_specs, check_vma=False)
```

profile of v0, /device:TPU:1, one launch (start us, length us, event | category | flops | bytes accessed | tf_op | source)
XLA Modules:
  0.0 1212.6 jit_solution(16224556508730017022)
XLA Ops:
  7.2 8.7 reduce.8
  19.7 180.5 %all-reduce.10.cloned.1.call-done = f32[192,192]{1,0:T(8,128)} async-done(((f32[192,192]{1,0:T(8,128)}), f32[192,192]{1,0:T(8,128)}) %all-reduce.10.cloned.1.call-update) | async-done | bytes 147472 | tf_op jit(solution)/shard_map/psum | solution.py:12
  203.0 11.7 cholesky.182
  214.8 9.8 custom-call.15
  226.7 5.9 cholesky.202
  236.0 20.3 %custom-call.16 = f32[2,128,128]{1,2,0:T(8,128)} custom-call(f32[2,128,128]{2,1,0:T(8,128)S(1)} %pad_maximum_fusion), custom_call_target="InvertDiagBlocksLowerTriangular" | custom-call | tf_op jit(solution)/shard_map/triangular_solve/custom-call.0 | solution.py:40
  260.4 44.9 %all-reduce.12.cloned.1.call-done = f32[1,192,192]{2,1,0:T(8,128)} async-done(((f32[1,192,192]{2,1,0:T(8,128)}), f32[1,192,192]{2,1,0:T(8,128)}) %all-reduce.12.cloned.1.call-update) | async-done | bytes 147472 | tf_op jit(solution)/shard_map/psum | solution.py:12
  308.0 93.4 %all-gather.7.cloned.1.call-done = f32[64,192,192]{2,1,0:T(8,128)} async-done(((f32[1,192,192]{2,1,0:T(8,128)}), f32[64,192,192]{2,1,0:T(8,128)}) %all-gather.7.cloned.1.call-update) | async-done | bytes 9437200 | tf_op jit(solution)/shard_map/all_gather | solution.py:44
  401.4 5.5 bitcast_subtract_fusion.2
  413.4 172.8 %all-reduce.14.cloned.1.call-done = f32[192,192]{1,0:T(8,128)} async-done(((f32[192,192]{1,0:T(8,128)}), f32[192,192]{1,0:T(8,128)}) %all-reduce.14.cloned.1.call-update) | async-done | bytes 147472 | tf_op jit(solution)/shard_map/psum | solution.py:12
  589.0 12.3 %cholesky.220 = f32[128,128]{1,0:T(8,128)} custom-call(f32[128,128]{1,0:T(8,128)S(1)} %copy.78), custom_call_target="Cholesky" | custom-call | tf_op jit(solution)/shard_map/jit(cholesky)/cholesky | solution.py:39
  603.6 11.3 custom-call.17
  619.1 7.2 cholesky.240
  631.8 21.1 %custom-call.18 = f32[2,128,128]{1,2,0:T(8,128)} custom-call(f32[2,128,128]{2,1,0:T(8,128)} %pad_maximum_fusion.1), custom_call_target="InvertDiagBlocksLowerTriangular" | custom-call | tf_op jit(solution)/shard_map/triangular_solve/custom-call.0 | solution.py:40
  656.7 44.9 %all-reduce.16.cloned.1.call-done = f32[1,192,192]{2,1,0:T(8,128)} async-done(((f32[1,192,192]{2,1,0:T(8,128)}), f32[1,192,192]{2,1,0:T(8,128)}) %all-reduce.16.cloned.1.call-update) | async-done | bytes 147472 | tf_op jit(solution)/shard_map/psum | solution.py:12
  701.9 95.2 %all-gather.9.cloned.1.call-done = f32[64,192,192]{2,1,0:T(8,128)} async-done(((f32[1,192,192]{2,1,0:T(8,128)}), f32[64,192,192]{2,1,0:T(8,128)}) %all-gather.9.cloned.1.call-update) | async-done | bytes 9437200 | tf_op jit(solution)/shard_map/all_gather | solution.py:44
  797.1 4.8 bitcast_subtract_fusion.1
  806.7 173.5 %all-reduce.18.cloned.1.call-done = f32[192,192]{1,0:T(8,128)} async-done(((f32[192,192]{1,0:T(8,128)}), f32[192,192]{1,0:T(8,128)}) %all-reduce.18.cloned.1.call-update) | async-done | bytes 147472 | tf_op jit(solution)/shard_map/psum | solution.py:12
  983.0 12.3 %cholesky.258 = f32[128,128]{1,0:T(8,128)} custom-call(f32[128,128]{1,0:T(8,128)S(1)} %copy.89), custom_call_target="Cholesky" | custom-call | tf_op jit(solution)/shard_map/jit(cholesky)/cholesky | solution.py:39
  997.6 11.3 custom-call.19
  1013.0 7.2 cholesky.278
  1025.8 21.1 %custom-call.20 = f32[2,128,128]{1,2,0:T(8,128)} custom-call(f32[2,128,128]{2,1,0:T(8,128)} %pad_maximum_fusion.2), custom_call_target="InvertDiagBlocksLowerTriangular" | custom-call | tf_op jit(solution)/shard_map/triangular_solve/custom-call.0 | solution.py:40
  1050.9 44.7 %all-reduce.20.cloned.1.call-done = f32[1,192,192]{2,1,0:T(8,128)} async-done(((f32[1,192,192]{2,1,0:T(8,128)}), f32[1,192,192]{2,1,0:T(8,128)}) %all-reduce.20.cloned.1.call-update) | async-done | bytes 147472 | tf_op jit(solution)/shard_map/psum | solution.py:12
  1095.6 96.0 %all-gather.11.cloned.1.call-done = f32[64,192,192]{2,1,0:T(8,128)} async-done(((f32[1,192,192]{2,1,0:T(8,128)}), f32[64,192,192]{2,1,0:T(8,128)}) %all-gather.11.cloned.1.call-update) | async-done | bytes 9437200 | tf_op jit(solution)/shard_map/all_gather | solution.py:44
  (138 shorter events, 77.7 us)
Async XLA Ops:
  6.5 193.7 %all-reduce.10.cloned.1.call-start = ((), (), s32[]{:S(2)}) async-start(), calls=%async_computation | async-start | bytes 393216 | tf_op jit(solution)/shard_map/psum | solution.py:12
  19.5 285.9 %all-reduce.12.cloned.1.call-start = ((), (), s32[]{:S(2)}) async-start(), calls=%async_computation.1 | async-start | bytes 393216 | tf_op jit(solution)/shard_map/psum | solution.py:12
  19.7 285.7 %copy-start.6 = (f32[128,64]{1,0:T(8,128)}, f32[128,64]{1,0:T(8,128)S(1)}, u32[]{:S(2)}) copy-start(f32[128,64]{1,0:T(8,128)S(1)} %pad_convert_fusion) | copy-start | bytes 98308
  202.2 0.7 copy-start.8
  235.2 0.7 copy-start.10
  260.4 141.0 %all-gather.7.cloned.1.call-start = ((), (), s32[]{:S(2)}) async-start(), calls=%async_computation.6 | async-start | bytes 12779520 | tf_op jit(solution)/shard_map/all_gather | solution.py:44
  305.3 280.9 %all-reduce.14.cloned.1.call-start = ((), (), s32[]{:S(2)}) async-start(), calls=%async_computation.2 | async-start | bytes 393216 | tf_op jit(solution)/shard_map/psum | solution.py:12
  305.4 96.0 %copy-start.4 = (f32[1,192,192]{2,1,0:T(8,128)S(1)}, f32[1,192,192]{2,1,0:T(8,128)}, u32[]{:S(2)}) copy-start(f32[1,192,192]{2,1,0:T(8,128)} %all-reduce.12.cloned.1.call-done) | copy-start | bytes 442372
  412.9 288.7 %all-reduce.16.cloned.1.call-start = ((), (), s32[]{:S(2)}) async-start(), calls=%async_computation.3 | async-start | bytes 393216 | tf_op jit(solution)/shard_map/psum | solution.py:12
  588.2 0.7 copy-start.9
  629.5 0.7 copy-start.12
  656.7 140.5 %all-gather.9.cloned.1.call-start = ((), (), s32[]{:S(2)}) async-start(), calls=%async_computation.7 | async-start | bytes 12779520 | tf_op jit(solution)/shard_map/all_gather | solution.py:44
  701.6 278.5 %all-reduce.18.cloned.1.call-start = ((), (), s32[]{:S(2)}) async-start(), calls=%async_computation.4 | async-start | bytes 393216 | tf_op jit(solution)/shard_map/psum | solution.py:12
  797.1 6.6 copy-start.3
  802.0 1.7 copy-start
  804.7 387.0 %copy-start.1 = (f32[1,16,192,192]{2,3,1,0:T(8,128)S(1)}, f32[1,16,192,192]{2,3,1,0:T(8,128)}, u32[]{:S(2)}) copy-start(f32[1,16,192,192]{2,3,1,0:T(8,128)} %constant_dynamic-update-slice_fusion.4) | copy-start | bytes 7077892
  806.6 289.0 %all-reduce.20.cloned.1.call-start = ((), (), s32[]{:S(2)}) async-start(), calls=%async_computation.5 | async-start | bytes 393216 | tf_op jit(solution)/shard_map/psum | solution.py:12
  982.2 0.7 copy-start.7
  1023.5 0.7 copy-start.11
  1050.7 141.0 %all-gather.11.cloned.1.call-start = ((), (), s32[]{:S(2)}) async-start(), calls=%async_computation.8 | async-start | bytes 12779520 | tf_op jit(solution)/shard_map/all_gather | solution.py:44
  1191.7 6.6 copy-start.5
  1196.5 1.7 copy-start.2
Sparse Core Ops, SparseCore 0:
  19.6 180.5 all-reduce.9
  260.5 44.7 all-reduce.11
  308.4 92.8 all-gather.6
  413.0 173.1 all-reduce.13
  656.8 44.7 all-reduce.15
  704.2 92.8 all-gather.8
  806.7 173.3 all-reduce.17
  1050.8 44.7 all-reduce.19
  1098.7 92.8 all-gather.10
where the time goes:
time: 1220 us; the launch traced here: 1210 us
  waiting for transfers between devices  946 us (78%)
  other arithmetic  181 us (15%)
  local copies, waits for them, and re-layouts  34 us (3%)
  matrix products  32 us (3%)
  between operations  18.5 us (2%)
    psum x6, waiting for transfers between devices, from_root(): return lax.psum(jnp.where(mine, array, jnp.zeros_like(array)), axis)  661 us
    all_gather x3, waiting for transfers between devices, body(): every = lax.all_gather(panel_tiles[:, None], 'row', axis=1, tiled=True)  285 us
    another operation x21, other arithmetic, body(): factor = jnp.linalg.cholesky(block)  97.4 us
    another operation x14, other arithmetic, body(): lax.linalg.triangular_solve(factor, flat_column, left_side=False, lower=T...  65.8 us
  transfers between devices with their start and end apart: 9, of which 9 were waited for; matrix products, arithmetic and copies ran while one was open for 0% of the time, Pallas kernels for 0%

commit v1 on v0

v1 whole, which is shorter than its diff:
```python
import jax
import jax.numpy as jnp
from jax import lax
from jax.experimental import pallas as pl
from jax.experimental.pallas import tpu as pltpu
from jax.sharding import PartitionSpec as P

B = 192
BLK = 32
SUB = 16
HIGH = lax.Precision.HIGHEST
F32 = jnp.float32
BF16 = jnp.bfloat16


def lanes_below(n, shape):
    return lax.broadcasted_iota(jnp.int32, shape, 1) < n


def unflatten(get, dst):
    f0, f1, f2 = get(0), get(1), get(2)
    low = lanes_below(64, f0.shape)
    zero = jnp.zeros_like(f0)
    dst[0, pl.ds(0, 96, stride=2), :] = f0
    dst[1, pl.ds(0, 96, stride=2), :] = jnp.where(low, f1, zero)
    dst[0, pl.ds(1, 96, stride=2), :] = pltpu.roll(jnp.where(low, f2, f1), 64, 1)
    dst[1, pl.ds(1, 96, stride=2), :] = jnp.where(low, pltpu.roll(f2, 64, 1), zero)


def load(ref, rows=B):
    return jnp.concatenate([ref[0, 0:rows, :], ref[1, 0:rows, :]], axis=1)


def store(ref, value):
    ref[0, 0:B, :] = value[:, :128]
    ref[1, 0:B, :] = value[:, 128:]


def flatten(even, odd):
    e0, e1 = even[:, :128], even[:, 128:]
    o0, o1 = odd[:, :128], odd[:, 128:]
    low = lanes_below(64, e0.shape)
    return e0, jnp.where(low, e1, pltpu.roll(o0, 64, 1)), pltpu.roll(jnp.where(low, o1, o0), 64, 1)


def split3(u):
    h = u.astype(BF16)
    rest = u - h.astype(F32)
    m = rest.astype(BF16)
    return h, m, (rest - m.astype(F32)).astype(BF16)


def split2(u):
    h = u.astype(BF16)
    return h, (u - h.astype(F32)).astype(BF16)


def factor_block(sa, r0):
    lo = 128 * (r0 // 128)
    hi = 384 if r0 + BLK <= 128 else 512
    width = hi - lo
    tiles = width // 128
    rows = sa[r0:r0 + BLK, lo:hi]
    diag = jnp.ones((BLK, 128), F32)
    ids = lax.broadcasted_iota(jnp.int32, (BLK, 128), 0)
    for sub in range(BLK // SUB):
        top = sub * SUB
        height = BLK - top
        live = rows[top:, :]
        col0 = r0 + top - lo
        cols = [jnp.broadcast_to(live[:, col0 + i:col0 + i + 1], (height, 128)) for i in range(SUB)]
        sub_ids = lax.broadcasted_iota(jnp.int32, (height, 128), 0)
        for j in range(SUB):
            cj = cols[j]
            pivot = cj[j:j + 1, :]
            f = jnp.where(sub_ids > j, cj * (1.0 / pivot), 0.0)
            diag = jnp.where(ids == top + j, pivot, diag)
            for i in range(j + 1, SUB):
                cols[i] = cols[i] - f * cj[i:i + 1, :]
            wide = jnp.concatenate([f] * tiles, axis=1)
            live = live - wide * live[j:j + 1, :]
        rows = live if top == 0 else jnp.concatenate([rows[:top], live], axis=0)
    u = rows * jnp.concatenate([lax.rsqrt(diag)] * tiles, axis=1)
    sa[r0:r0 + BLK, lo:hi] = u
    if r0 + BLK < B:
        h, m, l = split3(u)
        left = jnp.concatenate([h, h, m, h, m, l], axis=0)[:, :256 - lo]
        right = jnp.concatenate([h, m, h, l, m, h], axis=0)
        change = lax.dot_general(left, right, (((0,), (0,)), ((), ())), preferred_element_type=F32)
        sa[r0 + BLK:B, lo:hi] = sa[r0 + BLK:B, lo:hi] - change[r0 + BLK - lo:B - lo]


def start_tile(sa):
    r = lax.broadcasted_iota(jnp.int32, (B, 256), 0)
    c = lax.broadcasted_iota(jnp.int32, (B, 256), 1)
    sa[:, 256:512] = jnp.where(r == c, 1.0, 0.0).astype(F32)


def finish_tile(sa, linv, lfac):
    r = lax.broadcasted_iota(jnp.int32, (B, 256), 0)
    c = lax.broadcasted_iota(jnp.int32, (B, 256), 1)
    linv[0:B, :] = sa[:, 256:512]
    linv[B:256, :] = jnp.zeros((256 - B, 256), F32)
    u = jnp.where(r <= c, sa[:, 0:256], 0.0)
    full = jnp.concatenate([u, jnp.zeros((64, 256), F32)], axis=0)
    lfac[...] = full.T[0:B, :]


def nt(a, b):
    return lax.dot_general(a, b, (((1,), (1,)), ((), ())), precision=HIGH, preferred_element_type=F32)


def nn(a, b):
    return jnp.dot(a, b, precision=HIGH, preferred_element_type=F32)


def panel_step(t, g, linv, live):
    for p in range(t, 3):
        x = nt(load(g.at[t, p]), linv[t])
        if p == 2:
            x = jnp.where(live[t], x, 0.0)
        store(g.at[t, p], x)
    for s in range(t + 1, 3):
        for p in range(s - 1, 3):
            store(g.at[s, p], load(g.at[s, p]) - nt(load(g.at[t, p]), load(g.at[t, s - 1], 256)))


def weights(g, linv, w, whi, wlo):
    def full(t, p):
        return load(g.at[t, p], 256)

    w2 = nn(load(g.at[2, 2]), linv[2])
    w1 = nn(load(g.at[1, 2]) - nn(w2, full(1, 1)), linv[1])
    w0 = nn(load(g.at[0, 2]) - nn(w2, full(0, 1)) - nn(w1, full(0, 0)), linv[0])
    for t, v in enumerate((w0, w1, w2)):
        store(w.at[t], v)
    for half in range(2):
        v = jnp.concatenate([w[i // 2, i % 2, pl.ds(half, 96, stride=2), :] for i in range(6)], axis=1)
        whi[96 * half:96 * half + 96, :], wlo[96 * half:96 * half + 96, :] = split2(v)


def special_tile(special, flat, g, lfac, which, same):
    x = jnp.where(which == 0, load(g.at[0, 2]), jnp.where(which == 1, load(g.at[1, 2]), load(g.at[2, 2])))
    f = jnp.where(which == 0, lfac[0], jnp.where(which == 1, lfac[1], lfac[2]))
    store(special, jnp.where(same, f, x))
    even = jnp.concatenate([special[i, pl.ds(0, 96, stride=2), :] for i in range(2)], axis=1)
    odd = jnp.concatenate([special[i, pl.ds(1, 96, stride=2), :] for i in range(2)], axis=1)
    for i, v in enumerate(flatten(even, odd)):
        flat[pl.ds(i, 96, stride=3), :] = v


def update(c, matrix, out, panel_get, bt, whi, wlo, flat, j, panel, which, take):
    for t in range(3):
        unflatten(panel_get(c, t), bt.at[t])
    bhi, blo = split2(jnp.concatenate([bt[i // 2, i % 2] for i in range(6)], axis=1))
    dims = (((1,), (1,)), ((), ()))
    change = lax.dot_general(whi[...], bhi, dims, preferred_element_type=F32)
    change = change + lax.dot_general(wlo[...], bhi, dims, preferred_element_type=F32)
    change = change + lax.dot_general(whi[...], blo, dims, preferred_element_type=F32)
    change = jnp.concatenate([change, jnp.zeros((B, 64), F32)], axis=1)
    change = jnp.where(j > panel, change, 0.0)
    use = jnp.logical_and(take, j == panel + which)
    for i, v in enumerate(flatten(change[0:96], change[96:192])):
        old = matrix[c, pl.ds(i, 96, stride=3), :]
        out[c, pl.ds(i, 96, stride=3), :] = jnp.where(use, flat[pl.ds(i, 96, stride=3), :], old - v)


MESH = pl.DeviceIdType.MESH
N_SEM = 96


def kernel(
    panel_ref, matrix, out,
    rel, own, mask1, got1, sum1, gotz1, sum2, goty1, tile1,
    mask2, got2, sum3, gotz2, tile2, app, panels,
    sa, linv, lfac, g, w, whi, wlo, bt, special, flat,
    send_sem, recv_sem,
):
    panel = panel_ref[0]
    my_row, my_col = lax.axis_index("row"), lax.axis_index("col")
    x, z, core = my_row // 16, (my_row // 2) % 8, my_row % 2
    eight = 2 * x + core
    pair = my_row % 4
    which = lax.rem(my_col - panel + 64, 4)

    def at_y(d):
        return {"row": my_row, "col": (my_col + d) % 4}

    def at_eight(d):
        e = (eight + d) % 8
        return {"row": 16 * (e // 2) + 2 * z + e % 2, "col": my_col}

    def at_x(d):
        return {"row": (my_row + 16 * d) % 64, "col": my_col}

    def at_z(d):
        return {"row": 16 * x + 2 * ((z + d) % 8) + core, "col": my_col}

    def at_pair(u):
        return {"row": my_row - pair + u, "col": my_col}

    other_core = {"row": my_row - core + (1 - core), "col": my_col}
    count = [0]
    sent = []

    def copy(src, dst, device, start=True):
        i = count[0]
        count[0] += 1
        c = pltpu.make_async_remote_copy(
            src_ref=src, dst_ref=dst, send_sem=send_sem.at[i], recv_sem=recv_sem.at[i],
            device_id=device, device_id_type=MESH,
        )
        if start:
            c.start()
            sent.append(c)
        return c

    def arrive(copies):
        for c in copies:
            c.wait_recv()

    barrier = pltpu.get_barrier_semaphore()
    near = [at_y(d) for d in range(1, 4)] + [at_eight(d) for d in range(1, 8)] + [at_z(d) for d in range(1, 8)]
    near.append(at_pair(3 - pair))
    for device in near:
        pl.semaphore_signal(barrier, inc=1, device_id=device, device_id_type=MESH)

    slot = jnp.minimum((panel + which) // 4, 15)
    mine = matrix[slot]
    rel[0] = mine
    first = jnp.where(jnp.logical_and(my_row == panel, which == 0), mine, 0.0)
    for i in range(8):
        mask1[i] = first[36 * i:36 * i + 36]
    g[...] = jnp.zeros_like(g)
    pl.semaphore_wait(barrier, len(near))

    state = {}

    def start():
        state["first"] = [copy(mask1.at[(eight + d) % 8], got1.at[d], at_eight(d)) for d in range(1, 8)]
        state["y"] = [copy(rel.at[0], rel.at[d], at_y(d)) for d in range(1, 4)]

    def first_z():
        arrive(state["first"])
        total = mask1[eight]
        for d in range(1, 8):
            total = total + got1[d]
        sum1[...] = total
        state["first"] = [copy(sum1, gotz1.at[d], at_z(d)) for d in range(1, 8)]

    def first_y():
        arrive(state["first"])
        total = sum1[...]
        for d in range(1, 8):
            total = total + gotz1[d]
        sum2[...] = total
        state["first"] = [copy(sum2, goty1.at[d], at_y(d)) for d in range(1, 4)]

    def first_gather():
        arrive(state["first"])
        total = sum2[...]
        for d in range(1, 4):
            total = total + goty1[d]
        tile1[eight] = total
        state["first"] = [copy(tile1.at[eight], tile1.at[eight], at_eight(d)) for d in range(1, 8)]

    def first_done():
        arrive(state["first"])
        for i in range(8):
            app[0, 36 * i:36 * i + 36, :] = tile1[i]

    order = [(1, 0), (1, 1), (2, 0), (2, 1), (2, 2)]

    def row_ready():
        arrive(state["y"])
        for t in range(3):
            own[288 * t:288 * t + 288, :] = rel[(my_col - panel - t + 64) % 4]

    def rest_start():
        for n, (s, t) in enumerate(order):
            v = own[pl.ds(pl.multiple_of(288 * t + 72 * my_col, 8), 72), :]
            v = jnp.where(my_row == panel + s, v, 0.0)
            for i in range(8):
                mask2[i, n] = v[9 * i:9 * i + 9]
        state["rest"] = [copy(mask2.at[(eight + d) % 8], got2.at[d], at_eight(d)) for d in range(1, 8)]

    def rest_z():
        arrive(state["rest"])
        total = mask2[eight]
        for d in range(1, 8):
            total = total + got2[d]
        sum3[...] = total
        state["rest"] = [copy(sum3, gotz2.at[d], at_z(d)) for d in range(1, 8)]

    def rest_gather():
        arrive(state["rest"])
        total = sum3[...]
        for d in range(1, 8):
            total = total + gotz2[d]
        tile2[my_col, eight] = total
        mine = tile2.at[my_col, eight]
        state["rest"] = [copy(mine, mine, at_eight(d)) for d in range(1, 8)]

    def rest_y():
        arrive(state["rest"])
        state["rest"] = [copy(tile2.at[my_col], tile2.at[my_col], at_y(d)) for d in range(1, 4)]

    def rest_done():
        arrive(state["rest"])
        for n in range(5):
            for q in range(4):
                for i in range(8):
                    row = 72 * q + 9 * i
                    app[n + 1, row:row + 9, :] = tile2[q, i, n]

    def spread():
        base = pl.multiple_of(216 * pair, 8)
        copies = []
        for d in range(1, 4):
            u = (pair + d) % 4
            copies.append(copy(
                own.at[pl.ds(pl.multiple_of(216 * u, 8), 216)], panels.at[x, 2 * (z // 2) + u // 2, u % 2],
                at_pair(u), start=False,
            ))

        @pl.when(pair == my_col)
        def _():
            for c in copies:
                c.start()
            panels[x, z, core] = own[pl.ds(base, 216), :]

        state["spread"] = copies

    def spread_done():
        for d in range(1, 4):
            @pl.when((pair - d + 4) % 4 == my_col)
            def _():
                state["spread"][d - 1].wait_recv()

        here = panels.at[x, z, core]
        state["x"] = [copy(here, here, at_x(d)) for d in range(1, 4)]

    def ring(step):
        def block(d):
            return panels.at[:, (z + d) % 8, core]

        def half(d, h):
            return panels.at[pl.ds(2 * h, 2), (z + d) % 8, core]

        if step == 0:
            arrive(state["x"])
            state["core"] = []
        else:
            arrive(state["ring"])
        if step < 3:
            state["ring"] = [copy(block(-step), block(-step), at_z(1)), copy(block(step), block(step), at_z(-1))]
        elif step == 3:
            state["ring"] = [copy(half(-3, 0), half(-3, 0), at_z(1)), copy(half(3, 1), half(3, 1), at_z(-1))]
        for d in ([0] if step == 0 else [-step, step] if step < 4 else [4]):
            state["core"].append(copy(block(d), block(d), other_core))

    def ring_done():
        arrive(state["core"])

    def flat_rows(ref, *idx):
        return lambda o: ref[(*idx, pl.ds(o, 96, stride=3), slice(None))]

    def panel_rows(c, t):
        return lambda o: panel_rows_of(c, t, o)

    def panel_rows_of(c, t, o):
        parts, row, end = [], 288 * t, 288 * t + 288
        while row < end:
            u = row // 216
            stop = min(end, 216 * u + 216)
            parts.append(panels[c // 4, 2 * (c % 4) + u // 2, u % 2, pl.ds(row - 216 * u + o, (stop - row) // 3, stride=3), :])
            row = stop
        return jnp.concatenate(parts, axis=0)

    live = [my_row > panel + t for t in range(3)]
    comm = {
        (0, 0): [spread_done], (0, 1): [rest_z], (0, 2): [lambda: ring(0)], (0, 3): [rest_gather], (0, 4): [rest_y],
        (1, 0): [lambda: ring(1)], (1, 3): [lambda: ring(2)], (2, 0): [lambda: ring(3)], (2, 3): [lambda: ring(4)],
    }

    start()
    first_z()
    first_y()
    row_ready()
    rest_start()
    first_gather()
    spread()
    for t in range(3):
        unflatten(lambda o, t=t: own[pl.ds(288 * t + o, 96, stride=3), :], g.at[t, 2])
    first_done()
    unflatten(flat_rows(app, 0), bt.at[0])
    for t in range(3):
        sa[:, 0:256] = load(bt.at[0]) if t == 0 else load(g.at[t, t - 1])
        start_tile(sa)
        for blk in range(6):
            factor_block(sa, BLK * blk)
            for phase in comm.get((t, blk), []):
                phase()
        if t == 0:
            rest_done()
            for n, place in enumerate([(0, 0), (1, 0), (0, 1), (1, 1), (2, 1)]):
                unflatten(flat_rows(app, n + 1), g.at[place])
        finish_tile(sa, linv.at[t], lfac.at[t])
        panel_step(t, g, linv, live)
    weights(g, linv, w, whi, wlo)
    tile = panel + which
    special_tile(special, flat, g, lfac, which, my_row == tile)
    take = jnp.logical_and(which < 3, my_row >= tile)
    ring_done()

    def one(c, carry):
        update(c, matrix, out, panel_rows, bt, whi, wlo, flat, 4 * c + my_col, panel, which, take)
        return carry

    lax.fori_loop(0, 16, one, 0)
    for c in sent:
        c.wait_send()

    @pl.when(pair == my_col)
    def _():
        for c in state["spread"]:
            c.wait_send()


def body(matrix, panel_index):
    flat = matrix.reshape(16, 288, 128)
    V = pltpu.VMEM
    scratch = [
        V((4, 288, 128), F32), V((864, 128), F32), V((8, 36, 128), F32), V((8, 36, 128), F32), V((36, 128), F32),
        V((8, 36, 128), F32), V((36, 128), F32), V((4, 36, 128), F32), V((8, 36, 128), F32),
        V((8, 5, 9, 128), F32), V((8, 5, 9, 128), F32), V((5, 9, 128), F32), V((8, 5, 9, 128), F32),
        V((4, 8, 5, 9, 128), F32), V((6, 288, 128), F32), V((4, 8, 2, 216, 128), F32),
        V((B, 512), F32), V((3, 256, 256), F32), V((3, B, 256), F32), V((3, 3, 2, 256, 128), F32),
        V((3, 2, B, 128), F32), V((B, 768), BF16), V((B, 768), BF16), V((3, 2, B, 128), F32), V((2, B, 128), F32),
        V((288, 128), F32),
        pltpu.SemaphoreType.DMA((N_SEM,)), pltpu.SemaphoreType.DMA((N_SEM,)),
    ]
    out = pl.pallas_call(
        kernel,
        out_shape=jax.ShapeDtypeStruct((16, 288, 128), F32),
        in_specs=[pl.BlockSpec(memory_space=pltpu.SMEM), pl.BlockSpec(memory_space=pltpu.VMEM)],
        out_specs=pl.BlockSpec(memory_space=pltpu.VMEM),
        scratch_shapes=scratch,
        compiler_params=pltpu.CompilerParams(collective_id=0, has_side_effects=True, vmem_limit_bytes=48 << 20),
        name="panel_steps",
    )(panel_index, flat)
    return out.reshape(matrix.shape)


def solution(mesh):
    in_specs = (P(None, "row", None, "col", None), P())
    out_specs = P(None, "row", None, "col", None)
    return jax.shard_map(body, mesh=mesh, in_specs=in_specs, out_specs=out_specs, check_vma=False)
```

time: 1220 us -> 100 us (0.08)
  waiting for transfers between devices: 946 us -> 0 us
  other arithmetic: 181 us -> 0 us
  Pallas kernels: 0 us -> 95.6 us
  matrix products: 32 us -> 0 us
  local copies, waits for them, and re-layouts: 34 us -> 3.07 us
  between operations: 18.5 us -> 0.67 us
    psum x6 -> x0, waiting for transfers between devices: 661 us -> none  [from_root(): return lax.psum(jnp.where(mine, array, jnp.zeros_like(array)), axis)]
    all_gather x3 -> x0, waiting for transfers between devices: 285 us -> none  [body(): every = lax.all_gather(panel_tiles[:, None], 'row', axis=1, tiled=True)]
    another operation x35 -> x0, other arithmetic: 163 us -> none  [the longest x21 97.4 us: body(): factor = jnp.linalg.cholesky(block)]
    pallas_call x0 -> x1, Pallas kernels: none -> 95.6 us  [body(): pl.pallas_call(kernel, out_shape=jax.ShapeDtypeStruct((16, 288, 128), F32...]
    another operation x15 -> x0, matrix products: 16.8 us -> none  [the longest x9 9.4 us: body(): lax.linalg.triangular_solve(factor, flat_column, left_side=False, lower=T...]
    dot_general x3 -> x0, matrix products: 15.2 us -> none  [body(): jnp.einsum('rab,cdb->rcad', row_live, col_live, precision=lax.Precision.H...]
  transfers between devices with their start and end apart: 9 -> 0, of which waited for: 9 -> 0; matrix products, arithmetic and copies ran while one was open for 0% -> 0% of each run, Pallas kernels for 0% -> 0%
where the time goes in v1:
time: 100 us; the launch traced here: 99.3 us
  Pallas kernels  95.6 us (96%)
  local copies, waits for them, and re-layouts  3.07 us (3%)
    pallas_call x1, Pallas kernels, body(): pl.pallas_call(kernel, out_shape=jax.ShapeDtypeStruct((16, 288, 128), F32...  95.6 us
    unnamed x3, local copies, waits for them, and re-layouts  3.07 us

profile of v1, /device:TPU:1, one launch (start us, length us, event | category | flops | bytes accessed | tf_op | source)
XLA Modules:
  0.0 99.3 jit_solution(2189534325338870051)
XLA Ops:
  0.7 0.0 copy-start
  0.7 1.7 %copy-done = f32[1,1,16,1,36864]{4,3,2,1,0:T(1,128)S(1)} copy-done((f32[1,1,16,1,36864]{4,3,2,1,0:T(1,128)S(1)}, f32[1,1,16,1,36864]{4,3,2,1,0:T(1,128)}, u32[]{:S(2)}) %copy-start) | copy-done | bytes 2359320
  2.3 95.6 %panel_steps.1 = f32[16,288,128]{2,1,0:T(8,128)S(1)} custom-call(s32[1]{0:T(128)S(6)} %copy.5.panel_ref, f32[16,288,128]{2,1,0:T(8,128)S(1)} %bitcast.3), custom_call_target="tpu_custom_call" | custom-call | tf_op jit(solution)/shard_map/panel_steps/pallas_call | solution.py:443
  97.9 1.4 %copy.6 = f32[1,1,16,1,36864]{4,3,2,1,0:T(1,128)} copy(f32[1,1,16,1,36864]{4,3,2,1,0:T(1,128)S(1)} %bitcast.2) | data formatting | bytes 4718592
Async XLA Ops:
  0.7 1.7 %copy-start = (f32[1,1,16,1,36864]{4,3,2,1,0:T(1,128)S(1)}, f32[1,1,16,1,36864]{4,3,2,1,0:T(1,128)}, u32[]{:S(2)}) copy-start(f32[1,1,16,1,36864]{4,3,2,1,0:T(1,128)} %param.2) | copy-start | bytes 7077892

commit v2 on v1

v2 whole, which is shorter than its diff:
```python
import jax
import jax.numpy as jnp
from jax import lax
from jax.experimental import pallas as pl
from jax.experimental.pallas import tpu as pltpu
from jax.sharding import PartitionSpec as P

B = 192
BLK = 32
SUB = 16
HIGH = lax.Precision.HIGHEST
F32 = jnp.float32
BF16 = jnp.bfloat16


def lanes_below(n, shape):
    return lax.broadcasted_iota(jnp.int32, shape, 1) < n


def unflatten(get, dst):
    f0, f1, f2 = get(0), get(1), get(2)
    low = lanes_below(64, f0.shape)
    zero = jnp.zeros_like(f0)
    dst[0, pl.ds(0, 96, stride=2), :] = f0
    dst[1, pl.ds(0, 96, stride=2), :] = jnp.where(low, f1, zero)
    dst[0, pl.ds(1, 96, stride=2), :] = pltpu.roll(jnp.where(low, f2, f1), 64, 1)
    dst[1, pl.ds(1, 96, stride=2), :] = jnp.where(low, pltpu.roll(f2, 64, 1), zero)


def load(ref, rows=B):
    return jnp.concatenate([ref[0, 0:rows, :], ref[1, 0:rows, :]], axis=1)


def store(ref, value):
    ref[0, 0:B, :] = value[:, :128]
    ref[1, 0:B, :] = value[:, 128:]


def flatten(even, odd):
    e0, e1 = even[:, :128], even[:, 128:]
    o0, o1 = odd[:, :128], odd[:, 128:]
    low = lanes_below(64, e0.shape)
    return e0, jnp.where(low, e1, pltpu.roll(o0, 64, 1)), pltpu.roll(jnp.where(low, o1, o0), 64, 1)


def split3(u):
    h = u.astype(BF16)
    rest = u - h.astype(F32)
    m = rest.astype(BF16)
    return h, m, (rest - m.astype(F32)).astype(BF16)


def split2(u):
    h = u.astype(BF16)
    return h, (u - h.astype(F32)).astype(BF16)


def factor_block(sa, r0):
    lo = 128 * (r0 // 128)
    hi = 384 if r0 + BLK <= 128 else 512
    width = hi - lo
    tiles = width // 128
    rows = sa[r0:r0 + BLK, lo:hi]
    diag = jnp.ones((BLK, 128), F32)
    ids = lax.broadcasted_iota(jnp.int32, (BLK, 128), 0)
    for sub in range(BLK // SUB):
        top = sub * SUB
        height = BLK - top
        live = rows[top:, :]
        col0 = r0 + top - lo
        cols = [jnp.broadcast_to(live[:, col0 + i:col0 + i + 1], (height, 128)) for i in range(SUB)]
        sub_ids = lax.broadcasted_iota(jnp.int32, (height, 128), 0)
        for j in range(SUB):
            cj = cols[j]
            pivot = cj[j:j + 1, :]
            f = jnp.where(sub_ids > j, cj * (1.0 / pivot), 0.0)
            diag = jnp.where(ids == top + j, pivot, diag)
            for i in range(j + 1, SUB):
                cols[i] = cols[i] - f * cj[i:i + 1, :]
            wide = jnp.concatenate([f] * tiles, axis=1)
            live = live - wide * live[j:j + 1, :]
        rows = live if top == 0 else jnp.concatenate([rows[:top], live], axis=0)
    u = rows * jnp.concatenate([lax.rsqrt(diag)] * tiles, axis=1)
    sa[r0:r0 + BLK, lo:hi] = u
    if r0 + BLK < B:
        h, m, l = split3(u)
        left = jnp.concatenate([h, h, m, h, m, l], axis=0)[:, :256 - lo]
        right = jnp.concatenate([h, m, h, l, m, h], axis=0)
        change = lax.dot_general(left, right, (((0,), (0,)), ((), ())), preferred_element_type=F32)
        sa[r0 + BLK:B, lo:hi] = sa[r0 + BLK:B, lo:hi] - change[r0 + BLK - lo:B - lo]


def start_tile(sa):
    r = lax.broadcasted_iota(jnp.int32, (B, 256), 0)
    c = lax.broadcasted_iota(jnp.int32, (B, 256), 1)
    sa[:, 256:512] = jnp.where(r == c, 1.0, 0.0).astype(F32)


def finish_tile(sa, linv, lfac):
    r = lax.broadcasted_iota(jnp.int32, (B, 256), 0)
    c = lax.broadcasted_iota(jnp.int32, (B, 256), 1)
    linv[0:B, :] = sa[:, 256:512]
    linv[B:256, :] = jnp.zeros((256 - B, 256), F32)
    u = jnp.where(r <= c, sa[:, 0:256], 0.0)
    full = jnp.concatenate([u, jnp.zeros((64, 256), F32)], axis=0)
    lfac[...] = full.T[0:B, :]


def nt(a, b):
    return lax.dot_general(a, b, (((1,), (1,)), ((), ())), precision=HIGH, preferred_element_type=F32)


def nn(a, b):
    return jnp.dot(a, b, precision=HIGH, preferred_element_type=F32)


def panel_step(t, g, linv, live):
    for p in range(t, 3):
        x = nt(load(g.at[t, p]), linv[t])
        if p == 2:
            x = jnp.where(live[t], x, 0.0)
        store(g.at[t, p], x)
    for s in range(t + 1, 3):
        for p in range(s - 1, 3):
            store(g.at[s, p], load(g.at[s, p]) - nt(load(g.at[t, p]), load(g.at[t, s - 1], 256)))


def weights(g, linv, w, whi, wlo):
    def full(t, p):
        return load(g.at[t, p], 256)

    w2 = nn(load(g.at[2, 2]), linv[2])
    w1 = nn(load(g.at[1, 2]) - nn(w2, full(1, 1)), linv[1])
    w0 = nn(load(g.at[0, 2]) - nn(w2, full(0, 1)) - nn(w1, full(0, 0)), linv[0])
    for t, v in enumerate((w0, w1, w2)):
        store(w.at[t], v)
    for half in range(2):
        v = jnp.concatenate([w[i // 2, i % 2, pl.ds(half, 96, stride=2), :] for i in range(6)], axis=1)
        whi[96 * half:96 * half + 96, :], wlo[96 * half:96 * half + 96, :] = split2(v)


def special_tile(special, flat, g, lfac, which, same):
    x = jnp.where(which == 0, load(g.at[0, 2]), jnp.where(which == 1, load(g.at[1, 2]), load(g.at[2, 2])))
    f = jnp.where(which == 0, lfac[0], jnp.where(which == 1, lfac[1], lfac[2]))
    store(special, jnp.where(same, f, x))
    even = jnp.concatenate([special[i, pl.ds(0, 96, stride=2), :] for i in range(2)], axis=1)
    odd = jnp.concatenate([special[i, pl.ds(1, 96, stride=2), :] for i in range(2)], axis=1)
    for i, v in enumerate(flatten(even, odd)):
        flat[pl.ds(i, 96, stride=3), :] = v


def update(c, matrix, out, panel_get, bt, whi, wlo, flat, j, panel, which, take):
    for t in range(3):
        unflatten(panel_get(c, t), bt.at[t])
    bhi, blo = split2(jnp.concatenate([bt[i // 2, i % 2] for i in range(6)], axis=1))
    dims = (((1,), (1,)), ((), ()))
    change = lax.dot_general(whi[...], bhi, dims, preferred_element_type=F32)
    change = change + lax.dot_general(wlo[...], bhi, dims, preferred_element_type=F32)
    change = change + lax.dot_general(whi[...], blo, dims, preferred_element_type=F32)
    change = jnp.concatenate([change, jnp.zeros((B, 64), F32)], axis=1)
    change = jnp.where(j > panel, change, 0.0)
    use = jnp.logical_and(take, j == panel + which)
    for i, v in enumerate(flatten(change[0:96], change[96:192])):
        old = matrix[c, pl.ds(i, 96, stride=3), :]
        out[c, pl.ds(i, 96, stride=3), :] = jnp.where(use, flat[pl.ds(i, 96, stride=3), :], old - v)


MESH = pl.DeviceIdType.MESH
N_SEM = 256
ORDER = [(0, 0), (1, 0), (1, 1), (2, 0), (2, 1), (2, 2)]
GROUPS = [(0, 1), (1, 2), (3, 3)]
LONG, SHORT = 48, 24


def kernel(
    panel_ref, matrix, out,
    cut, got, pick, gotz0, gotz1, gotz2, tile0, tile1, tile2, rel, own, app, fresh, main, side,
    sa, linv, lfac, g, w, whi, wlo, bt, special, flat,
    send_sem, recv_sem, quarter_sem, fresh_sem,
):
    panel = panel_ref[0]
    my_row, my_col = lax.axis_index("row"), lax.axis_index("col")
    x, z, core = my_row // 16, (my_row // 2) % 8, my_row % 2
    which = lax.rem(my_col - panel + 64, 4)
    gathered = [tile0, tile1, tile2]
    gotz = [gotz0, gotz1, gotz2]

    def at(dx, dc, dy, dz=0):
        c = core if dc == 0 else 1 - core
        return {"row": 16 * ((x + dx) % 4) + 2 * ((z + dz) % 8) + c, "col": (my_col + dy) % 4}

    def at_quarter(u):
        return {"row": 16 * x + 2 * (2 * (z // 2) + u // 2) + u % 2, "col": my_row % 4}

    group = [(dx, dc, dy) for dc in range(2) for dx in range(4) for dy in range(4)][1:]
    count = [0]
    sent = []

    def copy(src, dst, device):
        i = count[0]
        count[0] += 1
        c = pltpu.make_async_remote_copy(
            src_ref=src, dst_ref=dst, send_sem=send_sem.at[i], recv_sem=recv_sem.at[i],
            device_id=device, device_id_type=MESH,
        )
        c.start()
        sent.append(c)
        return c

    def arrive(copies):
        for c in copies:
            c.wait_recv()

    barrier = pltpu.get_barrier_semaphore()
    near = [at(*d) for d in group] + [at(0, 0, 0, dz) for dz in range(1, 8)]
    across = 2 * (z // 2) + 1 - z % 2
    for dc in range(2):
        for dy in range(4):
            if dc or dy:
                near.append({"row": 16 * x + 2 * across + (core if dc == 0 else 1 - core), "col": (my_col + dy) % 4})
    for device in near:
        pl.semaphore_signal(barrier, inc=1, device_id=device, device_id_type=MESH)

    slot = jnp.minimum((panel + which) // 4, 15)
    mine = matrix[slot]
    rel[0] = mine
    for i in range(32):
        cut[i // 16, (i // 4) % 4, i % 4] = mine[9 * i:9 * i + 9]
    g[...] = jnp.zeros_like(g)
    got[x, core, my_col] = cut[core, x, my_col]
    pl.semaphore_wait(barrier, len(near))

    pieces = []
    for dx, dc, dy in group:
        c = core if dc == 0 else 1 - core
        pieces.append(copy(
            cut.at[c, (x + dx) % 4, (my_col + dy) % 4], got.at[x, core, my_col], at(dx, dc, dy),
        ))
    state = {}
    here = 2 * (z % 2) + core
    to_me = here == my_col
    quarters = []

    def send_quarters():
        for d in range(4):
            u = (here + d) % 4
            part = rel.at[0, pl.ds(pl.multiple_of(72 * u, 8), 72)]
            quarters.append(pltpu.make_async_remote_copy(
                src_ref=part, dst_ref=fresh.at[my_col], send_sem=quarter_sem.at[d], recv_sem=fresh_sem.at[my_col],
                device_id=at_quarter(u), device_id_type=MESH,
            ))
        for c in quarters[1:]:
            c.start()

        @pl.when(jnp.logical_not(to_me))
        def _():
            quarters[0].start()

        @pl.when(to_me)
        def _():
            fresh[my_col] = rel[0, pl.ds(pl.multiple_of(72 * here, 8), 72), :]

    def quarters_ready():
        for q in range(4):
            c = pltpu.make_async_remote_copy(
                src_ref=rel.at[0, pl.ds(0, 72)], dst_ref=fresh.at[q], send_sem=quarter_sem.at[0], recv_sem=fresh_sem.at[q],
                device_id=at_quarter(0), device_id_type=MESH,
            )

            @pl.when(jnp.logical_not(jnp.logical_and(to_me, my_col == q)))
            def _():
                c.wait_recv()

    def quarters_sent():
        for c in quarters[1:]:
            c.wait_send()

        @pl.when(jnp.logical_not(to_me))
        def _():
            quarters[0].wait_send()

    def pick_rows():
        arrive(pieces)
        for n, (s, t) in enumerate(ORDER):
            r = panel + s
            pick[n] = got[r // 16, r % 2, (panel + t) % 4]
        state["z"] = []
        for (a, n), dst in zip(GROUPS, gotz):
            dst[z] = pick[a:a + n]
            state["z"].append([copy(pick.at[pl.ds(a, n)], dst.at[z], at(0, 0, 0, dz)) for dz in range(1, 8)])

    def gather(i):
        arrive(state["z"][i])
        a, n = GROUPS[i]
        tile = gathered[i]
        for m in range(n):
            r = panel + ORDER[a + m][0]
            tile[core, x, my_col, m] = gotz[i][(r // 2) % 8, m]
        here = tile.at[core, x, my_col]
        members = group if i == 0 else [d for d in group if d[1] == 0]
        state[i] = [copy(here, here, at(*d)) for d in members]

    def other_core(i):
        arrive(state[i])
        half = gathered[i].at[core]
        state[i] = [copy(half, half, at(0, 1, 0))]

    def placed(i):
        arrive(state[i])
        a, n = GROUPS[i]
        for m in range(n):
            for p in range(32):
                app[a + m, 9 * p:9 * p + 9, :] = gathered[i][p // 16, (p // 4) % 4, p % 4, m]

    def row_start():
        state["y"] = [copy(rel.at[0], rel.at[d], at(0, 0, d)) for d in range(1, 4)]

    def row_ready():
        arrive(state["y"])
        for t in range(3):
            own[t] = rel[(my_col - panel - t + 64) % 4]
            unflatten(lambda o, t=t: own[t, pl.ds(o, 96, stride=3), :], g.at[t, 2])

    def bulk_start():
        for t in range(3):
            v = fresh[(panel + t) % 4]
            main[x, z, core, t] = v[:LONG]
            side[x, z, core, t] = v[LONG:]
        a, b = main.at[x, z, core], side.at[x, z, core]
        state["b"] = [copy(b, b, at(d, 0, 0)) for d in range(1, 4)]
        state["a"] = {d: copy(a, a, at(0, 0, 0, d)) for d in (1, 7, 2, 6, 3, 5, 4)}
        state["ax"] = {0: [copy(a, a, at(d, 0, 0)) for d in range(1, 4)]}
        state["core"] = []

    def a_pass(*ds):
        for d in ds:
            state["a"][d].wait_recv()
            a = main.at[x, (z - d) % 8, core]
            state["ax"][d] = [copy(a, a, at(k, 0, 0)) for k in range(1, 4)]

    def a_core(*ds):
        for d in ds:
            arrive(state["ax"][d])
            a = main.at[:, (z - d) % 8, core]
            state["core"].append(copy(a, a, at(0, 1, 0)))

    def ring(step):
        def block(d):
            return side.at[:, (z + d) % 8, core]

        def half(d, h):
            return side.at[pl.ds(2 * h, 2), (z + d) % 8, core]

        arrive(state["b"])
        if step < 3:
            state["b"] = [copy(block(-step), block(-step), at(0, 0, 0, 1)), copy(block(step), block(step), at(0, 0, 0, -1))]
        elif step == 3:
            state["b"] = [copy(half(-3, 0), half(-3, 0), at(0, 0, 0, 1)), copy(half(3, 1), half(3, 1), at(0, 0, 0, -1))]
        for d in ([0] if step == 0 else [-step, step] if step < 4 else [4]):
            state["core"].append(copy(block(d), block(d), at(0, 1, 0)))

    def panel_rows(c, t):
        def rows(o):
            parts = []
            for u in range(4):
                place = (c // 4, 2 * (c % 4) + u // 2, u % 2, t)
                parts.append(main[(*place, pl.ds(o, LONG // 3, stride=3), slice(None))])
                parts.append(side[(*place, pl.ds(o, SHORT // 3, stride=3), slice(None))])
            return jnp.concatenate(parts, axis=0)

        return rows

    def app_tile(n, place):
        unflatten(lambda o: app[n, pl.ds(o, 96, stride=3), :], place)

    live = [my_row > panel + t for t in range(3)]
    agenda = {
        (0, 1): lambda: other_core(1), (0, 2): lambda: other_core(2), (0, 3): lambda: ring(0), (0, 4): lambda: a_pass(1, 7),
        (1, 0): lambda: a_pass(2, 6), (1, 1): lambda: ring(1), (1, 2): lambda: a_pass(3, 5), (1, 3): lambda: a_pass(4),
        (1, 4): lambda: ring(2), (2, 0): lambda: a_core(0, 1, 7), (2, 1): lambda: ring(3), (2, 2): lambda: a_core(2, 6),
        (2, 4): lambda: a_core(3), (2, 5): lambda: ring(4),
    }

    send_quarters()
    pick_rows()
    for i in range(3):
        gather(i)
    quarters_ready()
    bulk_start()
    row_start()
    placed(0)
    app_tile(0, bt.at[0])
    for t in range(3):
        sa[:, 0:256] = load(bt.at[0]) if t == 0 else load(g.at[t, t - 1])
        start_tile(sa)
        for blk in range(6):
            factor_block(sa, BLK * blk)
            if (t, blk) in agenda:
                agenda[(t, blk)]()
        finish_tile(sa, linv.at[t], lfac.at[t])
        if t == 0:
            placed(1)
            placed(2)
            for n, place in enumerate([(0, 0), (1, 0), (0, 1), (1, 1), (2, 1)]):
                app_tile(n + 1, g.at[place])
            row_ready()
        panel_step(t, g, linv, live)
    weights(g, linv, w, whi, wlo)
    tile = panel + which
    special_tile(special, flat, g, lfac, which, my_row == tile)
    take = jnp.logical_and(which < 3, my_row >= tile)
    a_core(5, 4)
    arrive(state["core"])

    def one(c, carry):
        update(c, matrix, out, panel_rows, bt, whi, wlo, flat, 4 * c + my_col, panel, which, take)
        return carry

    lax.fori_loop(0, 16, one, 0)
    for c in sent:
        c.wait_send()
    quarters_sent()


def body(matrix, panel_index):
    flat = matrix.reshape(16, 288, 128)
    V = pltpu.VMEM
    scratch = [
        V((2, 4, 4, 9, 128), F32), V((4, 2, 4, 9, 128), F32), V((6, 9, 128), F32), V((8, 1, 9, 128), F32), V((8, 2, 9, 128), F32), V((8, 3, 9, 128), F32),
        V((2, 4, 4, 1, 9, 128), F32), V((2, 4, 4, 2, 9, 128), F32), V((2, 4, 4, 3, 9, 128), F32),
        V((4, 288, 128), F32), V((3, 288, 128), F32), V((6, 288, 128), F32), V((4, 72, 128), F32),
        V((4, 8, 2, 3, LONG, 128), F32), V((4, 8, 2, 3, SHORT, 128), F32),
        V((B, 512), F32), V((3, 256, 256), F32), V((3, B, 256), F32), V((3, 3, 2, 256, 128), F32),
        V((3, 2, B, 128), F32), V((B, 768), BF16), V((B, 768), BF16), V((3, 2, B, 128), F32), V((2, B, 128), F32),
        V((288, 128), F32),
        pltpu.SemaphoreType.DMA((N_SEM,)), pltpu.SemaphoreType.DMA((N_SEM,)),
        pltpu.SemaphoreType.DMA((4,)), pltpu.SemaphoreType.DMA((4,)),
    ]
    out = pl.pallas_call(
        kernel,
        out_shape=jax.ShapeDtypeStruct((16, 288, 128), F32),
        in_specs=[pl.BlockSpec(memory_space=pltpu.SMEM), pl.BlockSpec(memory_space=pltpu.VMEM)],
        out_specs=pl.BlockSpec(memory_space=pltpu.VMEM),
        scratch_shapes=scratch,
        compiler_params=pltpu.CompilerParams(collective_id=0, has_side_effects=True, vmem_limit_bytes=48 << 20),
        name="panel_steps",
    )(panel_index, flat)
    return out.reshape(matrix.shape)


def solution(mesh):
    in_specs = (P(None, "row", None, "col", None), P())
    out_specs = P(None, "row", None, "col", None)
    return jax.shard_map(body, mesh=mesh, in_specs=in_specs, out_specs=out_specs, check_vma=False)
```

time: 100 us -> 80.2 us (0.80)
  Pallas kernels: 95.6 us -> 76.3 us
    pallas_call x1, Pallas kernels: 95.6 us -> 76.3 us  [body(): pl.pallas_call(kernel, out_shape=jax.ShapeDtypeStruct((16, 288, 128), F32...]
where the time goes in v2:
time: 80.2 us; the launch traced here: 80.1 us
  Pallas kernels  76.3 us (95%)
  local copies, waits for them, and re-layouts  3.07 us (4%)
    pallas_call x1, Pallas kernels, body(): pl.pallas_call(kernel, out_shape=jax.ShapeDtypeStruct((16, 288, 128), F32...  76.3 us
    unnamed x3, local copies, waits for them, and re-layouts  3.07 us

profile of v2, /device:TPU:1, one launch (start us, length us, event | category | flops | bytes accessed | tf_op | source)
XLA Modules:
  0.0 80.1 jit_solution(1572902165182424750)
XLA Ops:
  0.7 0.0 copy-start
  0.7 1.7 %copy-done = f32[1,1,16,1,36864]{4,3,2,1,0:T(1,128)S(1)} copy-done((f32[1,1,16,1,36864]{4,3,2,1,0:T(1,128)S(1)}, f32[1,1,16,1,36864]{4,3,2,1,0:T(1,128)}, u32[]{:S(2)}) %copy-start) | copy-done | bytes 2359320
  2.3 76.3 %panel_steps.1 = f32[16,288,128]{2,1,0:T(8,128)S(1)} custom-call(s32[1]{0:T(128)S(6)} %copy.5.panel_ref, f32[16,288,128]{2,1,0:T(8,128)S(1)} %bitcast.3), custom_call_target="tpu_custom_call" | custom-call | tf_op jit(solution)/shard_map/panel_steps/pallas_call | solution.py:439
  78.7 1.4 %copy.6 = f32[1,1,16,1,36864]{4,3,2,1,0:T(1,128)} copy(f32[1,1,16,1,36864]{4,3,2,1,0:T(1,128)S(1)} %bitcast.2) | data formatting | bytes 4718592
Async XLA Ops:
  0.7 1.7 %copy-start = (f32[1,1,16,1,36864]{4,3,2,1,0:T(1,128)S(1)}, f32[1,1,16,1,36864]{4,3,2,1,0:T(1,128)}, u32[]{:S(2)}) copy-start(f32[1,1,16,1,36864]{4,3,2,1,0:T(1,128)} %param.2) | copy-start | bytes 7077892

commit v3 on v2

--- a/solution.py
+++ b/solution.py
@@ -149,14 +149,16 @@
         flat[pl.ds(i, 96, stride=3), :] = v
 
 
-def update(c, matrix, out, panel_get, bt, whi, wlo, flat, j, panel, which, take):
+def convert(rows, bt, bhi, blo):
     for t in range(3):
-        unflatten(panel_get(c, t), bt.at[t])
-    bhi, blo = split2(jnp.concatenate([bt[i // 2, i % 2] for i in range(6)], axis=1))
+        unflatten(rows(t), bt.at[t])
+    bhi[...], blo[...] = split2(jnp.concatenate([bt[i // 2, i % 2] for i in range(6)], axis=1))
+
+
+def update(c, matrix, out, bhi, blo, whi, wlo, flat, j, panel, which, take):
     dims = (((1,), (1,)), ((), ()))
-    change = lax.dot_general(whi[...], bhi, dims, preferred_element_type=F32)
-    change = change + lax.dot_general(wlo[...], bhi, dims, preferred_element_type=F32)
-    change = change + lax.dot_general(whi[...], blo, dims, preferred_element_type=F32)
+    both = lax.dot_general(jnp.concatenate([whi[...], wlo[...]], axis=0), bhi[...], dims, preferred_element_type=F32)
+    change = both[:B] + both[B:] + lax.dot_general(whi[...], blo[...], dims, preferred_element_type=F32)
     change = jnp.concatenate([change, jnp.zeros((B, 64), F32)], axis=1)
     change = jnp.where(j > panel, change, 0.0)
     use = jnp.logical_and(take, j == panel + which)
@@ -169,14 +171,16 @@
 N_SEM = 256
 ORDER = [(0, 0), (1, 0), (1, 1), (2, 0), (2, 1), (2, 2)]
 GROUPS = [(0, 1), (1, 2), (3, 3)]
-LONG, SHORT = 48, 24
+LONG, SHORT = (48, 24, 48), (24, 48, 24)
+LONG_AT, SHORT_AT = (0, 48, 72), (0, 24, 72)
 
 
 def kernel(
-    panel_ref, matrix, out,
+    panel_ref, source, out,
+    matrix,
     cut, got, pick, gotz0, gotz1, gotz2, tile0, tile1, tile2, rel, own, app, fresh, main, side,
-    sa, linv, lfac, g, w, whi, wlo, bt, special, flat,
-    send_sem, recv_sem, quarter_sem, fresh_sem,
+    sa, linv, lfac, g, w, whi, wlo, bt, bhi, blo, special, flat,
+    matrix_sem, out_sem, send_sem, recv_sem, quarter_sem, fresh_sem,
 ):
     panel = panel_ref[0]
     my_row, my_col = lax.axis_index("row"), lax.axis_index("col")
@@ -211,6 +215,8 @@
         for c in copies:
             c.wait_recv()
 
+    fetch = pltpu.make_async_copy(source, matrix, matrix_sem)
+    fetch.start()
     barrier = pltpu.get_barrier_semaphore()
     near = [at(*d) for d in group] + [at(0, 0, 0, dz) for dz in range(1, 8)]
     across = 2 * (z // 2) + 1 - z % 2
@@ -221,12 +227,13 @@
     for device in near:
         pl.semaphore_signal(barrier, inc=1, device_id=device, device_id_type=MESH)
 
+    g[...] = jnp.zeros_like(g)
     slot = jnp.minimum((panel + which) // 4, 15)
+    fetch.wait()
     mine = matrix[slot]
     rel[0] = mine
     for i in range(32):
         cut[i // 16, (i // 4) % 4, i % 4] = mine[9 * i:9 * i + 9]
-    g[...] = jnp.zeros_like(g)
     got[x, core, my_col] = cut[core, x, my_col]
     pl.semaphore_wait(barrier, len(near))
 
@@ -321,30 +328,47 @@
             own[t] = rel[(my_col - panel - t + 64) % 4]
             unflatten(lambda o, t=t: own[t, pl.ds(o, 96, stride=3), :], g.at[t, 2])
 
+    def main_block(d):
+        return main.at[x, (z + d) % 8, core]
+
+    def pass_x(d):
+        state["ax"][d] = [copy(main_block(d), main_block(d), at(k, 0, 0)) for k in range(1, 4)]
+
     def bulk_start():
         for t in range(3):
             v = fresh[(panel + t) % 4]
-            main[x, z, core, t] = v[:LONG]
-            side[x, z, core, t] = v[LONG:]
-        a, b = main.at[x, z, core], side.at[x, z, core]
+            main[x, z, core, LONG_AT[t]:LONG_AT[t] + LONG[t], :] = v[:LONG[t]]
+            side[x, z, core, SHORT_AT[t]:SHORT_AT[t] + SHORT[t], :] = v[LONG[t]:]
+        state["core"], state["ax"] = [], {}
+        main_ring(0)
+        b = side.at[x, z, core]
         state["b"] = [copy(b, b, at(d, 0, 0)) for d in range(1, 4)]
-        state["a"] = {d: copy(a, a, at(0, 0, 0, d)) for d in (1, 7, 2, 6, 3, 5, 4)}
-        state["ax"] = {0: [copy(a, a, at(d, 0, 0)) for d in range(1, 4)]}
-        state["core"] = []
-
-    def a_pass(*ds):
-        for d in ds:
-            state["a"][d].wait_recv()
-            a = main.at[x, (z - d) % 8, core]
-            state["ax"][d] = [copy(a, a, at(k, 0, 0)) for k in range(1, 4)]
-
-    def a_core(*ds):
+
+    def main_ring(step):
+        def part(d, h):
+            return main.at[x, (z + d) % 8, core, pl.ds(64 * h, 64 - 8 * h)]
+
+        if step > 0:
+            arrive(state["a"])
+        if step < 3:
+            state["a"] = [
+                copy(main_block(-step), main_block(-step), at(0, 0, 0, 1)),
+                copy(main_block(step), main_block(step), at(0, 0, 0, -1)),
+            ]
+        elif step == 3:
+            state["a"] = [
+                copy(part(-3, 0), part(-3, 0), at(0, 0, 0, 1)), copy(part(3, 1), part(3, 1), at(0, 0, 0, -1)),
+            ]
+        for d in ([0] if step == 0 else [-step, step] if step < 4 else [4]):
+            pass_x(d)
+
+    def main_core(*ds):
         for d in ds:
             arrive(state["ax"][d])
-            a = main.at[:, (z - d) % 8, core]
+            a = main.at[:, (z + d) % 8, core]
             state["core"].append(copy(a, a, at(0, 1, 0)))
 
-    def ring(step):
+    def side_ring(step):
         def block(d):
             return side.at[:, (z + d) % 8, core]
 
@@ -363,9 +387,9 @@
         def rows(o):
             parts = []
             for u in range(4):
-                place = (c // 4, 2 * (c % 4) + u // 2, u % 2, t)
-                parts.append(main[(*place, pl.ds(o, LONG // 3, stride=3), slice(None))])
-                parts.append(side[(*place, pl.ds(o, SHORT // 3, stride=3), slice(None))])
+                place = (c // 4, 2 * (c % 4) + u // 2, u % 2)
+                parts.append(main[(*place, pl.ds(LONG_AT[t] + o, LONG[t] // 3, stride=3), slice(None))])
+                parts.append(side[(*place, pl.ds(SHORT_AT[t] + o, SHORT[t] // 3, stride=3), slice(None))])
             return jnp.concatenate(parts, axis=0)
 
         return rows
@@ -375,23 +399,25 @@
 
     live = [my_row > panel + t for t in range(3)]
     agenda = {
-        (0, 1): lambda: other_core(1), (0, 2): lambda: other_core(2), (0, 3): lambda: ring(0), (0, 4): lambda: a_pass(1, 7),
-        (1, 0): lambda: a_pass(2, 6), (1, 1): lambda: ring(1), (1, 2): lambda: a_pass(3, 5), (1, 3): lambda: a_pass(4),
-        (1, 4): lambda: ring(2), (2, 0): lambda: a_core(0, 1, 7), (2, 1): lambda: ring(3), (2, 2): lambda: a_core(2, 6),
-        (2, 4): lambda: a_core(3), (2, 5): lambda: ring(4),
+        (0, 0): lambda: other_core(1), (0, 1): lambda: other_core(2), (0, 2): lambda: main_ring(2),
+        (0, 4): lambda: side_ring(1), (1, 0): lambda: main_ring(3), (1, 2): lambda: side_ring(2),
+        (1, 3): lambda: main_ring(4), (1, 5): lambda: main_core(0, -1, 1), (2, 0): lambda: side_ring(3),
+        (2, 2): lambda: main_core(-2, 2), (2, 4): lambda: side_ring(4), (2, 5): lambda: main_core(-3, 3),
     }
 
     send_quarters()
     pick_rows()
+    quarters_ready()
+    bulk_start()
     for i in range(3):
         gather(i)
-    quarters_ready()
-    bulk_start()
     row_start()
+    main_ring(1)
+    side_ring(0)
     placed(0)
-    app_tile(0, bt.at[0])
+    app_tile(0, bt.at[0, 0])
     for t in range(3):
-        sa[:, 0:256] = load(bt.at[0]) if t == 0 else load(g.at[t, t - 1])
+        sa[:, 0:256] = load(bt.at[0, 0]) if t == 0 else load(g.at[t, t - 1])
         start_tile(sa)
         for blk in range(6):
             factor_block(sa, BLK * blk)
@@ -409,14 +435,24 @@
     tile = panel + which
     special_tile(special, flat, g, lfac, which, my_row == tile)
     take = jnp.logical_and(which < 3, my_row >= tile)
-    a_core(5, 4)
+    main_core(4)
     arrive(state["core"])
 
     def one(c, carry):
-        update(c, matrix, out, panel_rows, bt, whi, wlo, flat, 4 * c + my_col, panel, which, take)
+        for i in range(4):
+            convert(lambda t, i=i: panel_rows(4 * c + i, t), bt.at[i], bhi.at[i], blo.at[i])
+        for i in range(4):
+            j = 4 * (4 * c + i) + my_col
+            update(4 * c + i, matrix, matrix, bhi.at[i], blo.at[i], whi, wlo, flat, j, panel, which, take)
+        back(c).start()
         return carry
 
-    lax.fori_loop(0, 16, one, 0)
+    def back(c):
+        return pltpu.make_async_copy(matrix.at[pl.ds(4 * c, 4)], out.at[pl.ds(4 * c, 4)], out_sem.at[c])
+
+    lax.fori_loop(0, 4, one, 0)
+    for c in range(4):
+        back(c).wait()
     for c in sent:
         c.wait_send()
     quarters_sent()
@@ -426,23 +462,25 @@
     flat = matrix.reshape(16, 288, 128)
     V = pltpu.VMEM
     scratch = [
+        V((16, 288, 128), F32),
         V((2, 4, 4, 9, 128), F32), V((4, 2, 4, 9, 128), F32), V((6, 9, 128), F32), V((8, 1, 9, 128), F32), V((8, 2, 9, 128), F32), V((8, 3, 9, 128), F32),
         V((2, 4, 4, 1, 9, 128), F32), V((2, 4, 4, 2, 9, 128), F32), V((2, 4, 4, 3, 9, 128), F32),
         V((4, 288, 128), F32), V((3, 288, 128), F32), V((6, 288, 128), F32), V((4, 72, 128), F32),
-        V((4, 8, 2, 3, LONG, 128), F32), V((4, 8, 2, 3, SHORT, 128), F32),
+        V((4, 8, 2, sum(LONG), 128), F32), V((4, 8, 2, sum(SHORT), 128), F32),
         V((B, 512), F32), V((3, 256, 256), F32), V((3, B, 256), F32), V((3, 3, 2, 256, 128), F32),
-        V((3, 2, B, 128), F32), V((B, 768), BF16), V((B, 768), BF16), V((3, 2, B, 128), F32), V((2, B, 128), F32),
-        V((288, 128), F32),
+        V((3, 2, B, 128), F32), V((B, 768), BF16), V((B, 768), BF16), V((4, 3, 2, B, 128), F32),
+        V((4, B, 768), BF16), V((4, B, 768), BF16), V((2, B, 128), F32), V((288, 128), F32), pltpu.SemaphoreType.DMA,
+        pltpu.SemaphoreType.DMA((4,)),
         pltpu.SemaphoreType.DMA((N_SEM,)), pltpu.SemaphoreType.DMA((N_SEM,)),
         pltpu.SemaphoreType.DMA((4,)), pltpu.SemaphoreType.DMA((4,)),
     ]
     out = pl.pallas_call(
         kernel,
         out_shape=jax.ShapeDtypeStruct((16, 288, 128), F32),
-        in_specs=[pl.BlockSpec(memory_space=pltpu.SMEM), pl.BlockSpec(memory_space=pltpu.VMEM)],
-        out_specs=pl.BlockSpec(memory_space=pltpu.VMEM),
+        in_specs=[pl.BlockSpec(memory_space=pltpu.SMEM), pl.BlockSpec(memory_space=pltpu.HBM)],
+        out_specs=pl.BlockSpec(memory_space=pltpu.HBM),
         scratch_shapes=scratch,
-        compiler_params=pltpu.CompilerParams(collective_id=0, has_side_effects=True, vmem_limit_bytes=48 << 20),
+        compiler_params=pltpu.CompilerParams(collective_id=0, has_side_effects=True, vmem_limit_bytes=60 << 20),
         name="panel_steps",
     )(panel_index, flat)
     return out.reshape(matrix.shape)

time: 80.2 us -> 73 us (0.910)
  Pallas kernels: 76.3 us -> 69 us
    pallas_call x1, Pallas kernels: 76.3 us -> 69 us  [body(): pl.pallas_call(kernel, out_shape=jax.ShapeDtypeStruct((16, 288, 128), F32...]
    unnamed x3 -> x1, local copies, waits for them, and re-layouts: 3.07 us -> 3.24 us
where the time goes in v3:
time: 73 us; the launch traced here: 72.9 us
  Pallas kernels  69 us (95%)
  local copies, waits for them, and re-layouts  3.24 us (4%)
    pallas_call x1, Pallas kernels, body(): pl.pallas_call(kernel, out_shape=jax.ShapeDtypeStruct((16, 288, 128), F32...  69 us
    unnamed x1, local copies, waits for them, and re-layouts  3.24 us

profile of v3, /device:TPU:1, one launch (start us, length us, event | category | flops | bytes accessed | tf_op | source)
XLA Modules:
  0.0 72.9 jit_solution(550157233050692487)
XLA Ops:
  0.7 69.0 %panel_steps.1 = f32[16,288,128]{2,1,0:T(8,128)} custom-call(s32[1]{0:T(128)S(6)} %copy.5.panel_ref, f32[16,288,128]{2,1,0:T(8,128)} %bitcast.3), custom_call_target="tpu_custom_call" | custom-call | tf_op jit(solution)/shard_map/panel_steps/pallas_call | solution.py:477
  69.6 3.2 %copy.6 = f32[1,1,16,1,36864]{4,3,2,1,0:T(1,128)} copy(f32[1,1,16,1,36864]{4,3,2,1,0:T(1,128)} %bitcast.2) | data formatting | bytes 4718592

commit v4 on v3

--- a/solution.py
+++ b/solution.py
@@ -114,15 +114,19 @@
     return jnp.dot(a, b, precision=HIGH, preferred_element_type=F32)
 
 
-def panel_step(t, g, linv, live):
-    for p in range(t, 3):
-        x = nt(load(g.at[t, p]), linv[t])
-        if p == 2:
-            x = jnp.where(live[t], x, 0.0)
-        store(g.at[t, p], x)
+def panel_step(t, g, linv):
+    for p in range(t, 2):
+        store(g.at[t, p], nt(load(g.at[t, p]), linv[t]))
     for s in range(t + 1, 3):
-        for p in range(s - 1, 3):
+        for p in range(s - 1, 2):
             store(g.at[s, p], load(g.at[s, p]) - nt(load(g.at[t, p]), load(g.at[t, s - 1], 256)))
+
+
+def own_step(t, g, linv, live):
+    v = jnp.where(live[t], nt(load(g.at[t, 2]), linv[t]), 0.0)
+    store(g.at[t, 2], v)
+    for s in range(t + 1, 3):
+        store(g.at[s, 2], load(g.at[s, 2]) - nt(v, load(g.at[t, s - 1], 256)))
 
 
 def weights(g, linv, w, whi, wlo):
@@ -176,11 +180,10 @@
 
 
 def kernel(
-    panel_ref, source, out,
-    matrix,
+    panel_ref, matrix, out,
     cut, got, pick, gotz0, gotz1, gotz2, tile0, tile1, tile2, rel, own, app, fresh, main, side,
     sa, linv, lfac, g, w, whi, wlo, bt, bhi, blo, special, flat,
-    matrix_sem, out_sem, send_sem, recv_sem, quarter_sem, fresh_sem,
+    send_sem, recv_sem, quarter_sem, fresh_sem,
 ):
     panel = panel_ref[0]
     my_row, my_col = lax.axis_index("row"), lax.axis_index("col")
@@ -215,8 +218,6 @@
         for c in copies:
             c.wait_recv()
 
-    fetch = pltpu.make_async_copy(source, matrix, matrix_sem)
-    fetch.start()
     barrier = pltpu.get_barrier_semaphore()
     near = [at(*d) for d in group] + [at(0, 0, 0, dz) for dz in range(1, 8)]
     across = 2 * (z // 2) + 1 - z % 2
@@ -229,7 +230,6 @@
 
     g[...] = jnp.zeros_like(g)
     slot = jnp.minimum((panel + which) // 4, 15)
-    fetch.wait()
     mine = matrix[slot]
     rel[0] = mine
     for i in range(32):
@@ -342,7 +342,9 @@
         state["core"], state["ax"] = [], {}
         main_ring(0)
         b = side.at[x, z, core]
-        state["b"] = [copy(b, b, at(d, 0, 0)) for d in range(1, 4)]
+        state["b"] = {}
+        state["bx"] = {d: copy(b, b, at(d, 0, 0)) for d in range(1, 4)}
+        side_ring(0, 0)
 
     def main_ring(step):
         def part(d, h):
@@ -368,20 +370,33 @@
             a = main.at[:, (z + d) % 8, core]
             state["core"].append(copy(a, a, at(0, 1, 0)))
 
-    def side_ring(step):
-        def block(d):
-            return side.at[:, (z + d) % 8, core]
-
-        def half(d, h):
-            return side.at[pl.ds(2 * h, 2), (z + d) % 8, core]
-
-        arrive(state["b"])
-        if step < 3:
-            state["b"] = [copy(block(-step), block(-step), at(0, 0, 0, 1)), copy(block(step), block(step), at(0, 0, 0, -1))]
-        elif step == 3:
-            state["b"] = [copy(half(-3, 0), half(-3, 0), at(0, 0, 0, 1)), copy(half(3, 1), half(3, 1), at(0, 0, 0, -1))]
-        for d in ([0] if step == 0 else [-step, step] if step < 4 else [4]):
-            state["core"].append(copy(block(d), block(d), at(0, 1, 0)))
+    def side_ring(step, *ks):
+        def block(k, d):
+            return side.at[(x + k) % 4, (z + d) % 8, core]
+
+        def half(k, d, h):
+            return side.at[(x + k) % 4, (z + d) % 8, core, pl.ds(48 * h, 48)]
+
+        for k in ks:
+            if step > 0:
+                arrive(state["b"][k])
+            elif k > 0:
+                arrive([state["bx"][4 - k]])
+            if step < 3:
+                state["b"][k] = [
+                    copy(block(k, -step), block(k, -step), at(0, 0, 0, 1)),
+                    copy(block(k, step), block(k, step), at(0, 0, 0, -1)),
+                ]
+            elif step == 3:
+                state["b"][k] = [
+                    copy(half(k, -3, 0), half(k, -3, 0), at(0, 0, 0, 1)),
+                    copy(half(k, 3, 1), half(k, 3, 1), at(0, 0, 0, -1)),
+                ]
+
+    def side_core(*ds):
+        for d in ds:
+            a = side.at[:, (z + d) % 8, core]
+            state["core"].append(copy(a, a, at(0, 1, 0)))
 
     def panel_rows(c, t):
         def rows(o):
@@ -398,11 +413,18 @@
         unflatten(lambda o: app[n, pl.ds(o, 96, stride=3), :], place)
 
     live = [my_row > panel + t for t in range(3)]
+    rest = (1, 2, 3)
     agenda = {
-        (0, 0): lambda: other_core(1), (0, 1): lambda: other_core(2), (0, 2): lambda: main_ring(2),
-        (0, 4): lambda: side_ring(1), (1, 0): lambda: main_ring(3), (1, 2): lambda: side_ring(2),
-        (1, 3): lambda: main_ring(4), (1, 5): lambda: main_core(0, -1, 1), (2, 0): lambda: side_ring(3),
-        (2, 2): lambda: main_core(-2, 2), (2, 4): lambda: side_ring(4), (2, 5): lambda: main_core(-3, 3),
+        (0, 0): [lambda: other_core(1), lambda: other_core(2), row_start],
+        (0, 1): [lambda: side_ring(1, *rest), lambda: side_core(0)],
+        (0, 3): [lambda: main_ring(3), lambda: side_ring(3, 0)],
+        (1, 0): [lambda: side_ring(2, *rest), lambda: side_core(-1, 1)],
+        (1, 2): [lambda: main_ring(4), lambda: side_ring(4, 0)],
+        (1, 3): [lambda: main_core(0, -1, 1)],
+        (1, 5): [lambda: side_ring(3, *rest), lambda: side_core(-2, 2)],
+        (2, 1): [lambda: main_core(-2, 2)],
+        (2, 3): [lambda: main_core(-3, 3)],
+        (2, 4): [lambda: side_ring(4, *rest), lambda: side_core(-3, 3, 4)],
     }
 
     send_quarters()
@@ -411,9 +433,11 @@
     bulk_start()
     for i in range(3):
         gather(i)
-    row_start()
     main_ring(1)
-    side_ring(0)
+    side_ring(1, 0)
+    side_ring(0, *rest)
+    main_ring(2)
+    side_ring(2, 0)
     placed(0)
     app_tile(0, bt.at[0, 0])
     for t in range(3):
@@ -421,16 +445,20 @@
         start_tile(sa)
         for blk in range(6):
             factor_block(sa, BLK * blk)
-            if (t, blk) in agenda:
-                agenda[(t, blk)]()
+            for phase in agenda.get((t, blk), []):
+                phase()
         finish_tile(sa, linv.at[t], lfac.at[t])
         if t == 0:
             placed(1)
             placed(2)
             for n, place in enumerate([(0, 0), (1, 0), (0, 1), (1, 1), (2, 1)]):
                 app_tile(n + 1, g.at[place])
+        panel_step(t, g, linv)
+        if t == 1:
             row_ready()
-        panel_step(t, g, linv, live)
+            own_step(0, g, linv, live)
+        if t > 0:
+            own_step(t, g, linv, live)
     weights(g, linv, w, whi, wlo)
     tile = panel + which
     special_tile(special, flat, g, lfac, which, my_row == tile)
@@ -443,16 +471,10 @@
             convert(lambda t, i=i: panel_rows(4 * c + i, t), bt.at[i], bhi.at[i], blo.at[i])
         for i in range(4):
             j = 4 * (4 * c + i) + my_col
-            update(4 * c + i, matrix, matrix, bhi.at[i], blo.at[i], whi, wlo, flat, j, panel, which, take)
-        back(c).start()
+            update(4 * c + i, matrix, out, bhi.at[i], blo.at[i], whi, wlo, flat, j, panel, which, take)
         return carry
 
-    def back(c):
-        return pltpu.make_async_copy(matrix.at[pl.ds(4 * c, 4)], out.at[pl.ds(4 * c, 4)], out_sem.at[c])
-
     lax.fori_loop(0, 4, one, 0)
-    for c in range(4):
-        back(c).wait()
     for c in sent:
         c.wait_send()
     quarters_sent()
@@ -462,25 +484,23 @@
     flat = matrix.reshape(16, 288, 128)
     V = pltpu.VMEM
     scratch = [
-        V((16, 288, 128), F32),
         V((2, 4, 4, 9, 128), F32), V((4, 2, 4, 9, 128), F32), V((6, 9, 128), F32), V((8, 1, 9, 128), F32), V((8, 2, 9, 128), F32), V((8, 3, 9, 128), F32),
         V((2, 4, 4, 1, 9, 128), F32), V((2, 4, 4, 2, 9, 128), F32), V((2, 4, 4, 3, 9, 128), F32),
         V((4, 288, 128), F32), V((3, 288, 128), F32), V((6, 288, 128), F32), V((4, 72, 128), F32),
         V((4, 8, 2, sum(LONG), 128), F32), V((4, 8, 2, sum(SHORT), 128), F32),
         V((B, 512), F32), V((3, 256, 256), F32), V((3, B, 256), F32), V((3, 3, 2, 256, 128), F32),
         V((3, 2, B, 128), F32), V((B, 768), BF16), V((B, 768), BF16), V((4, 3, 2, B, 128), F32),
-        V((4, B, 768), BF16), V((4, B, 768), BF16), V((2, B, 128), F32), V((288, 128), F32), pltpu.SemaphoreType.DMA,
-        pltpu.SemaphoreType.DMA((4,)),
+        V((4, B, 768), BF16), V((4, B, 768), BF16), V((2, B, 128), F32), V((288, 128), F32),
         pltpu.SemaphoreType.DMA((N_SEM,)), pltpu.SemaphoreType.DMA((N_SEM,)),
         pltpu.SemaphoreType.DMA((4,)), pltpu.SemaphoreType.DMA((4,)),
     ]
     out = pl.pallas_call(
         kernel,
         out_shape=jax.ShapeDtypeStruct((16, 288, 128), F32),
-        in_specs=[pl.BlockSpec(memory_space=pltpu.SMEM), pl.BlockSpec(memory_space=pltpu.HBM)],
-        out_specs=pl.BlockSpec(memory_space=pltpu.HBM),
+        in_specs=[pl.BlockSpec(memory_space=pltpu.SMEM), pl.BlockSpec(memory_space=pltpu.VMEM)],
+        out_specs=pl.BlockSpec(memory_space=pltpu.VMEM),
         scratch_shapes=scratch,
-        compiler_params=pltpu.CompilerParams(collective_id=0, has_side_effects=True, vmem_limit_bytes=60 << 20),
+        compiler_params=pltpu.CompilerParams(collective_id=0, has_side_effects=True, vmem_limit_bytes=48 << 20),
         name="panel_steps",
     )(panel_index, flat)
     return out.reshape(matrix.shape)

time: 73 us -> 69.7 us (0.955)
  Pallas kernels: 69 us -> 65.8 us
    pallas_call x1, Pallas kernels: 69 us -> 65.8 us  [body(): pl.pallas_call(kernel, out_shape=jax.ShapeDtypeStruct((16, 288, 128), F32...]
    unnamed x1 -> x3, local copies, waits for them, and re-layouts: 3.24 us -> 3.07 us
where the time goes in v4:
time: 69.7 us; the launch traced here: 69.6 us
  Pallas kernels  65.8 us (94%)
  local copies, waits for them, and re-layouts  3.07 us (4%)
    pallas_call x1, Pallas kernels, body(): pl.pallas_call(kernel, out_shape=jax.ShapeDtypeStruct((16, 288, 128), F32...  65.8 us
    unnamed x3, local copies, waits for them, and re-layouts  3.07 us

profile of v4, /device:TPU:1, one launch (start us, length us, event | category | flops | bytes accessed | tf_op | source)
XLA Modules:
  0.0 69.6 jit_solution(18359768140234719692)
XLA Ops:
  0.7 0.0 copy-start
  0.7 1.7 %copy-done = f32[1,1,16,1,36864]{4,3,2,1,0:T(1,128)S(1)} copy-done((f32[1,1,16,1,36864]{4,3,2,1,0:T(1,128)S(1)}, f32[1,1,16,1,36864]{4,3,2,1,0:T(1,128)}, u32[]{:S(2)}) %copy-start) | copy-done | bytes 2359320
  2.3 65.8 %panel_steps.1 = f32[16,288,128]{2,1,0:T(8,128)S(1)} custom-call(s32[1]{0:T(128)S(6)} %copy.5.panel_ref, f32[16,288,128]{2,1,0:T(8,128)S(1)} %bitcast.3), custom_call_target="tpu_custom_call" | custom-call | tf_op jit(solution)/shard_map/panel_steps/pallas_call | solution.py:497
  68.2 1.4 %copy.6 = f32[1,1,16,1,36864]{4,3,2,1,0:T(1,128)} copy(f32[1,1,16,1,36864]{4,3,2,1,0:T(1,128)S(1)} %bitcast.2) | data formatting | bytes 4718592
Async XLA Ops:
  0.7 1.7 %copy-start = (f32[1,1,16,1,36864]{4,3,2,1,0:T(1,128)S(1)}, f32[1,1,16,1,36864]{4,3,2,1,0:T(1,128)}, u32[]{:S(2)}) copy-start(f32[1,1,16,1,36864]{4,3,2,1,0:T(1,128)} %param.2) | copy-start | bytes 7077892

commit v5 on v4

--- a/solution.py
+++ b/solution.py
@@ -175,8 +175,8 @@
 N_SEM = 256
 ORDER = [(0, 0), (1, 0), (1, 1), (2, 0), (2, 1), (2, 2)]
 GROUPS = [(0, 1), (1, 2), (3, 3)]
-LONG, SHORT = (48, 24, 48), (24, 48, 24)
-LONG_AT, SHORT_AT = (0, 48, 72), (0, 24, 72)
+LONG, SHORT = (48, 48, 48), (24, 24, 24)
+LONG_AT, SHORT_AT = (0, 48, 96), (0, 24, 48)
 
 
 def kernel(
@@ -187,17 +187,27 @@
 ):
     panel = panel_ref[0]
     my_row, my_col = lax.axis_index("row"), lax.axis_index("col")
-    x, z, core = my_row // 16, (my_row // 2) % 8, my_row % 2
+    x, core = lax.div(my_row, 16), lax.rem(my_row, 2)
+    z = lax.rem(lax.div(my_row, 2), 8)
+    xs = [x] + [lax.rem(x + d, 4) for d in range(1, 4)]
+    ys = [my_col] + [lax.rem(my_col + d, 4) for d in range(1, 4)]
+    zs = [z] + [lax.rem(z + d, 8) for d in range(1, 8)]
+    cs = [core, 1 - core]
+    x_rows, z_rows = [16 * v for v in xs], [2 * v for v in zs]
+    known = {}
+    here = lax.rem(my_row, 4)
     which = lax.rem(my_col - panel + 64, 4)
     gathered = [tile0, tile1, tile2]
     gotz = [gotz0, gotz1, gotz2]
 
     def at(dx, dc, dy, dz=0):
-        c = core if dc == 0 else 1 - core
-        return {"row": 16 * ((x + dx) % 4) + 2 * ((z + dz) % 8) + c, "col": (my_col + dy) % 4}
+        key = (dx, dc, dy, dz % 8)
+        if key not in known:
+            known[key] = {"row": x_rows[dx] + z_rows[dz % 8] + cs[dc], "col": ys[dy]}
+        return known[key]
 
     def at_quarter(u):
-        return {"row": 16 * x + 2 * (2 * (z // 2) + u // 2) + u % 2, "col": my_row % 4}
+        return {"row": my_row - here + u, "col": here}
 
     group = [(dx, dc, dy) for dc in range(2) for dx in range(4) for dy in range(4)][1:]
     count = [0]
@@ -220,11 +230,12 @@
 
     barrier = pltpu.get_barrier_semaphore()
     near = [at(*d) for d in group] + [at(0, 0, 0, dz) for dz in range(1, 8)]
-    across = 2 * (z // 2) + 1 - z % 2
+    z_half = lax.rem(z, 2)
+    across = z + 1 - 2 * z_half
     for dc in range(2):
         for dy in range(4):
             if dc or dy:
-                near.append({"row": 16 * x + 2 * across + (core if dc == 0 else 1 - core), "col": (my_col + dy) % 4})
+                near.append({"row": x_rows[0] + 2 * across + cs[dc], "col": ys[dy]})
     for device in near:
         pl.semaphore_signal(barrier, inc=1, device_id=device, device_id_type=MESH)
 
@@ -239,18 +250,16 @@
 
     pieces = []
     for dx, dc, dy in group:
-        c = core if dc == 0 else 1 - core
         pieces.append(copy(
-            cut.at[c, (x + dx) % 4, (my_col + dy) % 4], got.at[x, core, my_col], at(dx, dc, dy),
+            cut.at[cs[dc], xs[dx], ys[dy]], got.at[x, core, my_col], at(dx, dc, dy),
         ))
     state = {}
-    here = 2 * (z % 2) + core
     to_me = here == my_col
     quarters = []
 
     def send_quarters():
         for d in range(4):
-            u = (here + d) % 4
+            u = lax.rem(here + d, 4)
             part = rel.at[0, pl.ds(pl.multiple_of(72 * u, 8), 72)]
             quarters.append(pltpu.make_async_remote_copy(
                 src_ref=part, dst_ref=fresh.at[my_col], send_sem=quarter_sem.at[d], recv_sem=fresh_sem.at[my_col],
@@ -303,9 +312,9 @@
         for m in range(n):
             r = panel + ORDER[a + m][0]
             tile[core, x, my_col, m] = gotz[i][(r // 2) % 8, m]
-        here = tile.at[core, x, my_col]
+        mine = tile.at[core, x, my_col]
         members = group if i == 0 else [d for d in group if d[1] == 0]
-        state[i] = [copy(here, here, at(*d)) for d in members]
+        state[i] = [copy(mine, mine, at(*d)) for d in members]
 
     def other_core(i):
         arrive(state[i])
@@ -329,7 +338,7 @@
             unflatten(lambda o, t=t: own[t, pl.ds(o, 96, stride=3), :], g.at[t, 2])
 
     def main_block(d):
-        return main.at[x, (z + d) % 8, core]
+        return main.at[x, zs[d % 8], core]
 
     def pass_x(d):
         state["ax"][d] = [copy(main_block(d), main_block(d), at(k, 0, 0)) for k in range(1, 4)]
@@ -348,7 +357,7 @@
 
     def main_ring(step):
         def part(d, h):
-            return main.at[x, (z + d) % 8, core, pl.ds(64 * h, 64 - 8 * h)]
+            return main.at[x, zs[d % 8], core, pl.ds(72 * h, 72)]
 
         if step > 0:
             arrive(state["a"])
@@ -367,15 +376,15 @@
     def main_core(*ds):
         for d in ds:
             arrive(state["ax"][d])
-            a = main.at[:, (z + d) % 8, core]
+            a = main.at[:, zs[d % 8], core]
             state["core"].append(copy(a, a, at(0, 1, 0)))
 
     def side_ring(step, *ks):
         def block(k, d):
-            return side.at[(x + k) % 4, (z + d) % 8, core]
+            return side.at[xs[k], zs[d % 8], core]
 
         def half(k, d, h):
-            return side.at[(x + k) % 4, (z + d) % 8, core, pl.ds(48 * h, 48)]
+            return side.at[xs[k], zs[d % 8], core, pl.ds(40 * h, 40 - 8 * h)]
 
         for k in ks:
             if step > 0:
@@ -395,7 +404,7 @@
 
     def side_core(*ds):
         for d in ds:
-            a = side.at[:, (z + d) % 8, core]
+            a = side.at[:, zs[d % 8], core]
             state["core"].append(copy(a, a, at(0, 1, 0)))
 
     def panel_rows(c, t):
@@ -418,13 +427,11 @@
         (0, 0): [lambda: other_core(1), lambda: other_core(2), row_start],
         (0, 1): [lambda: side_ring(1, *rest), lambda: side_core(0)],
         (0, 3): [lambda: main_ring(3), lambda: side_ring(3, 0)],
-        (1, 0): [lambda: side_ring(2, *rest), lambda: side_core(-1, 1)],
+        (1, 1): [lambda: side_ring(2, *rest), lambda: side_core(-1, 1)],
         (1, 2): [lambda: main_ring(4), lambda: side_ring(4, 0)],
-        (1, 3): [lambda: main_core(0, -1, 1)],
-        (1, 5): [lambda: side_ring(3, *rest), lambda: side_core(-2, 2)],
-        (2, 1): [lambda: main_core(-2, 2)],
-        (2, 3): [lambda: main_core(-3, 3)],
-        (2, 4): [lambda: side_ring(4, *rest), lambda: side_core(-3, 3, 4)],
+        (1, 4): [lambda: main_core(0, -1, 1)],
+        (2, 2): [lambda: side_ring(3, *rest), lambda: side_core(-2, 2)],
+        (2, 4): [lambda: main_core(-2, 2)],
     }
 
     send_quarters()
@@ -463,7 +470,13 @@
     tile = panel + which
     special_tile(special, flat, g, lfac, which, my_row == tile)
     take = jnp.logical_and(which < 3, my_row >= tile)
+    main_core(-3, 3)
+    side_ring(4, *rest)
+    side_core(-3, 3, 4)
     main_core(4)
+    for c in sent:
+        c.wait_send()
+    quarters_sent()
     arrive(state["core"])
 
     def one(c, carry):
@@ -475,9 +488,6 @@
         return carry
 
     lax.fori_loop(0, 4, one, 0)
-    for c in sent:
-        c.wait_send()
-    quarters_sent()
 
 
 def body(matrix, panel_index):

time: 69.7 us -> 68.7 us (0.986)
  Pallas kernels: 65.8 us -> 64.9 us
    pallas_call x1, Pallas kernels: 65.8 us -> 64.9 us  [body(): pl.pallas_call(kernel, out_shape=jax.ShapeDtypeStruct((16, 288, 128), F32...]
where the time goes in v5:
time: 68.7 us; the launch traced here: 68.6 us
  Pallas kernels  64.9 us (94%)
  local copies, waits for them, and re-layouts  3.07 us (4%)
    pallas_call x1, Pallas kernels, body(): pl.pallas_call(kernel, out_shape=jax.ShapeDtypeStruct((16, 288, 128), F32...  64.9 us
    unnamed x3, local copies, waits for them, and re-layouts  3.07 us

profile of v5, /device:TPU:1, one launch (start us, length us, event | category | flops | bytes accessed | tf_op | source)
XLA Modules:
  0.0 68.6 jit_solution(4408124701995594722)
XLA Ops:
  0.7 0.0 copy-start
  0.7 1.7 %copy-done = f32[1,1,16,1,36864]{4,3,2,1,0:T(1,128)S(1)} copy-done((f32[1,1,16,1,36864]{4,3,2,1,0:T(1,128)S(1)}, f32[1,1,16,1,36864]{4,3,2,1,0:T(1,128)}, u32[]{:S(2)}) %copy-start) | copy-done | bytes 2359320
  2.3 64.9 %panel_steps.1 = f32[16,288,128]{2,1,0:T(8,128)S(1)} custom-call(s32[1]{0:T(128)S(6)} %copy.5.panel_ref, f32[16,288,128]{2,1,0:T(8,128)S(1)} %bitcast.3), custom_call_target="tpu_custom_call" | custom-call | tf_op jit(solution)/shard_map/panel_steps/pallas_call | solution.py:507
  67.2 1.4 %copy.6 = f32[1,1,16,1,36864]{4,3,2,1,0:T(1,128)} copy(f32[1,1,16,1,36864]{4,3,2,1,0:T(1,128)S(1)} %bitcast.2) | data formatting | bytes 4718592
Async XLA Ops:
  0.7 1.7 %copy-start = (f32[1,1,16,1,36864]{4,3,2,1,0:T(1,128)S(1)}, f32[1,1,16,1,36864]{4,3,2,1,0:T(1,128)}, u32[]{:S(2)}) copy-start(f32[1,1,16,1,36864]{4,3,2,1,0:T(1,128)} %param.2) | copy-start | bytes 7077892

commit v6 on v5

--- a/solution.py
+++ b/solution.py
@@ -174,14 +174,14 @@
 MESH = pl.DeviceIdType.MESH
 N_SEM = 256
 ORDER = [(0, 0), (1, 0), (1, 1), (2, 0), (2, 1), (2, 2)]
-GROUPS = [(0, 1), (1, 2), (3, 3)]
+GROUPS = [(0, 1), (1, 5)]
 LONG, SHORT = (48, 48, 48), (24, 24, 24)
 LONG_AT, SHORT_AT = (0, 48, 96), (0, 24, 48)
 
 
 def kernel(
     panel_ref, matrix, out,
-    cut, got, pick, gotz0, gotz1, gotz2, tile0, tile1, tile2, rel, own, app, fresh, main, side,
+    cut, got, pick, gotz0, gotz1, tile0, tile1, rel, own, app, fresh, main, side,
     sa, linv, lfac, g, w, whi, wlo, bt, bhi, blo, special, flat,
     send_sem, recv_sem, quarter_sem, fresh_sem,
 ):
@@ -197,8 +197,8 @@
     known = {}
     here = lax.rem(my_row, 4)
     which = lax.rem(my_col - panel + 64, 4)
-    gathered = [tile0, tile1, tile2]
-    gotz = [gotz0, gotz1, gotz2]
+    gathered = [tile0, tile1]
+    gotz = [gotz0, gotz1]
 
     def at(dx, dc, dy, dz=0):
         key = (dx, dc, dy, dz % 8)
@@ -313,8 +313,13 @@
             r = panel + ORDER[a + m][0]
             tile[core, x, my_col, m] = gotz[i][(r // 2) % 8, m]
         mine = tile.at[core, x, my_col]
-        members = group if i == 0 else [d for d in group if d[1] == 0]
+        members = [d for d in group if d[1] == 0 and (i == 0 or d[2] == 0)]
         state[i] = [copy(mine, mine, at(*d)) for d in members]
+
+    def rest_y():
+        arrive(state[1])
+        line = tile1.at[core, :, my_col]
+        state[1] = [copy(line, line, at(0, 0, d)) for d in range(1, 4)]
 
     def other_core(i):
         arrive(state[i])
@@ -424,9 +429,10 @@
     live = [my_row > panel + t for t in range(3)]
     rest = (1, 2, 3)
     agenda = {
-        (0, 0): [lambda: other_core(1), lambda: other_core(2), row_start],
+        (0, 0): [lambda: main_ring(2), lambda: side_ring(2, 0), row_start],
         (0, 1): [lambda: side_ring(1, *rest), lambda: side_core(0)],
-        (0, 3): [lambda: main_ring(3), lambda: side_ring(3, 0)],
+        (0, 4): [lambda: main_ring(3), lambda: side_ring(3, 0)],
+        (0, 5): [lambda: other_core(1)],
         (1, 1): [lambda: side_ring(2, *rest), lambda: side_core(-1, 1)],
         (1, 2): [lambda: main_ring(4), lambda: side_ring(4, 0)],
         (1, 4): [lambda: main_core(0, -1, 1)],
@@ -438,13 +444,13 @@
     pick_rows()
     quarters_ready()
     bulk_start()
-    for i in range(3):
-        gather(i)
+    gather(0)
+    gather(1)
     main_ring(1)
     side_ring(1, 0)
+    rest_y()
     side_ring(0, *rest)
-    main_ring(2)
-    side_ring(2, 0)
+    other_core(0)
     placed(0)
     app_tile(0, bt.at[0, 0])
     for t in range(3):
@@ -457,7 +463,6 @@
         finish_tile(sa, linv.at[t], lfac.at[t])
         if t == 0:
             placed(1)
-            placed(2)
             for n, place in enumerate([(0, 0), (1, 0), (0, 1), (1, 1), (2, 1)]):
                 app_tile(n + 1, g.at[place])
         panel_step(t, g, linv)
@@ -494,8 +499,8 @@
     flat = matrix.reshape(16, 288, 128)
     V = pltpu.VMEM
     scratch = [
-        V((2, 4, 4, 9, 128), F32), V((4, 2, 4, 9, 128), F32), V((6, 9, 128), F32), V((8, 1, 9, 128), F32), V((8, 2, 9, 128), F32), V((8, 3, 9, 128), F32),
-        V((2, 4, 4, 1, 9, 128), F32), V((2, 4, 4, 2, 9, 128), F32), V((2, 4, 4, 3, 9, 128), F32),
+        V((2, 4, 4, 9, 128), F32), V((4, 2, 4, 9, 128), F32), V((6, 9, 128), F32), V((8, 1, 9, 128), F32), V((8, 5, 9, 128), F32),
+        V((2, 4, 4, 1, 9, 128), F32), V((2, 4, 4, 5, 9, 128), F32),
         V((4, 288, 128), F32), V((3, 288, 128), F32), V((6, 288, 128), F32), V((4, 72, 128), F32),
         V((4, 8, 2, sum(LONG), 128), F32), V((4, 8, 2, sum(SHORT), 128), F32),
         V((B, 512), F32), V((3, 256, 256), F32), V((3, B, 256), F32), V((3, 3, 2, 256, 128), F32),

time: 68.7 us -> 69.7 us (1.015)
  Pallas kernels: 64.9 us -> 65.9 us
    pallas_call x1, Pallas kernels: 64.9 us -> 65.9 us  [body(): pl.pallas_call(kernel, out_shape=jax.ShapeDtypeStruct((16, 288, 128), F32...]
where the time goes in v6:
time: 69.7 us; the launch traced here: 69.6 us
  Pallas kernels  65.9 us (95%)
  local copies, waits for them, and re-layouts  3.07 us (4%)
    pallas_call x1, Pallas kernels, body(): pl.pallas_call(kernel, out_shape=jax.ShapeDtypeStruct((16, 288, 128), F32...  65.9 us
    unnamed x3, local copies, waits for them, and re-layouts  3.07 us

profile of v6, /device:TPU:1, one launch (start us, length us, event | category | flops | bytes accessed | tf_op | source)
XLA Modules:
  0.0 69.6 jit_solution(14295171034973837170)
XLA Ops:
  0.7 0.0 copy-start
  0.7 1.7 %copy-done = f32[1,1,16,1,36864]{4,3,2,1,0:T(1,128)S(1)} copy-done((f32[1,1,16,1,36864]{4,3,2,1,0:T(1,128)S(1)}, f32[1,1,16,1,36864]{4,3,2,1,0:T(1,128)}, u32[]{:S(2)}) %copy-start) | copy-done | bytes 2359320
  2.3 65.9 %panel_steps.1 = f32[16,288,128]{2,1,0:T(8,128)S(1)} custom-call(s32[1]{0:T(128)S(6)} %copy.5.panel_ref, f32[16,288,128]{2,1,0:T(8,128)S(1)} %bitcast.3), custom_call_target="tpu_custom_call" | custom-call | tf_op jit(solution)/shard_map/panel_steps/pallas_call | solution.py:512
  68.2 1.4 %copy.6 = f32[1,1,16,1,36864]{4,3,2,1,0:T(1,128)} copy(f32[1,1,16,1,36864]{4,3,2,1,0:T(1,128)S(1)} %bitcast.2) | data formatting | bytes 4718592
Async XLA Ops:
  0.7 1.7 %copy-start = (f32[1,1,16,1,36864]{4,3,2,1,0:T(1,128)S(1)}, f32[1,1,16,1,36864]{4,3,2,1,0:T(1,128)}, u32[]{:S(2)}) copy-start(f32[1,1,16,1,36864]{4,3,2,1,0:T(1,128)} %param.2) | copy-start | bytes 7077892

commit v7 on v5

--- a/solution.py
+++ b/solution.py
@@ -348,7 +348,7 @@
             v = fresh[(panel + t) % 4]
             main[x, z, core, LONG_AT[t]:LONG_AT[t] + LONG[t], :] = v[:LONG[t]]
             side[x, z, core, SHORT_AT[t]:SHORT_AT[t] + SHORT[t], :] = v[LONG[t]:]
-        state["core"], state["ax"] = [], {}
+        state["core"], state["ax"] = {}, {}
         main_ring(0)
         b = side.at[x, z, core]
         state["b"] = {}
@@ -377,7 +377,7 @@
         for d in ds:
             arrive(state["ax"][d])
             a = main.at[:, zs[d % 8], core]
-            state["core"].append(copy(a, a, at(0, 1, 0)))
+            state["core"][d] = [copy(a, a, at(0, 1, 0))] + state["core"].get(d, [])
 
     def side_ring(step, *ks):
         def block(k, d):
@@ -405,13 +405,17 @@
     def side_core(*ds):
         for d in ds:
             a = side.at[:, zs[d % 8], core]
-            state["core"].append(copy(a, a, at(0, 1, 0)))
-
-    def panel_rows(c, t):
+            state["core"][d] = [copy(a, a, at(0, 1, 0))] + state["core"].get(d, [])
+
+    def core_ready(*ds):
+        for d in ds:
+            arrive(state["core"][d])
+
+    def panel_rows(k, m, t):
         def rows(o):
             parts = []
             for u in range(4):
-                place = (c // 4, 2 * (c % 4) + u // 2, u % 2)
+                place = (k, 2 * m + u // 2, u % 2)
                 parts.append(main[(*place, pl.ds(LONG_AT[t] + o, LONG[t] // 3, stride=3), slice(None))])
                 parts.append(side[(*place, pl.ds(SHORT_AT[t] + o, SHORT[t] // 3, stride=3), slice(None))])
             return jnp.concatenate(parts, axis=0)
@@ -425,12 +429,12 @@
     rest = (1, 2, 3)
     agenda = {
         (0, 0): [lambda: other_core(1), lambda: other_core(2), row_start],
-        (0, 1): [lambda: side_ring(1, *rest), lambda: side_core(0)],
+        (0, 1): [lambda: side_ring(1, *rest), lambda: side_core(0, -1, 1)],
         (0, 3): [lambda: main_ring(3), lambda: side_ring(3, 0)],
-        (1, 1): [lambda: side_ring(2, *rest), lambda: side_core(-1, 1)],
+        (1, 1): [lambda: side_ring(2, *rest), lambda: side_core(-2, 2)],
         (1, 2): [lambda: main_ring(4), lambda: side_ring(4, 0)],
         (1, 4): [lambda: main_core(0, -1, 1)],
-        (2, 2): [lambda: side_ring(3, *rest), lambda: side_core(-2, 2)],
+        (2, 2): [lambda: side_ring(3, *rest), lambda: side_core(-3, 3)],
         (2, 4): [lambda: main_core(-2, 2)],
     }
 
@@ -470,24 +474,30 @@
     tile = panel + which
     special_tile(special, flat, g, lfac, which, my_row == tile)
     take = jnp.logical_and(which < 3, my_row >= tile)
+    half_z = lax.div(z, 2)
+
+    def columns(i):
+        m = lax.rem(half_z + i, 4)
+        for k in range(4):
+            convert(lambda t, k=k: panel_rows(k, m, t), bt.at[k], bhi.at[k], blo.at[k])
+        for k in range(4):
+            c = 4 * k + m
+            update(c, matrix, out, bhi.at[k], blo.at[k], whi, wlo, flat, 4 * c + my_col, panel, which, take)
+
     main_core(-3, 3)
+    core_ready(0, -1, 1)
+    columns(0)
     side_ring(4, *rest)
-    side_core(-3, 3, 4)
+    side_core(4)
     main_core(4)
+    core_ready(-2, 2, -3, 3)
+    columns(1)
+    columns(3)
     for c in sent:
         c.wait_send()
     quarters_sent()
-    arrive(state["core"])
-
-    def one(c, carry):
-        for i in range(4):
-            convert(lambda t, i=i: panel_rows(4 * c + i, t), bt.at[i], bhi.at[i], blo.at[i])
-        for i in range(4):
-            j = 4 * (4 * c + i) + my_col
-            update(4 * c + i, matrix, out, bhi.at[i], blo.at[i], whi, wlo, flat, j, panel, which, take)
-        return carry
-
-    lax.fori_loop(0, 4, one, 0)
+    core_ready(4)
+    columns(2)
 
 
 def body(matrix, panel_index):

time: 68.7 us -> 66.5 us (0.968)
  Pallas kernels: 64.9 us -> 62.7 us
    pallas_call x1, Pallas kernels: 64.9 us -> 62.7 us  [body(): pl.pallas_call(kernel, out_shape=jax.ShapeDtypeStruct((16, 288, 128), F32...]
where the time goes in v7:
time: 66.5 us; the launch traced here: 66.4 us
  Pallas kernels  62.7 us (94%)
  local copies, waits for them, and re-layouts  3.07 us (5%)
  between operations  0.67 us (1%)
    pallas_call x1, Pallas kernels, body(): pl.pallas_call(kernel, out_shape=jax.ShapeDtypeStruct((16, 288, 128), F32...  62.7 us
    unnamed x3, local copies, waits for them, and re-layouts  3.07 us

profile of v7, /device:TPU:1, one launch (start us, length us, event | category | flops | bytes accessed | tf_op | source)
XLA Modules:
  0.0 66.4 jit_solution(15575054152732355338)
XLA Ops:
  0.7 0.0 copy-start
  0.7 1.7 %copy-done = f32[1,1,16,1,36864]{4,3,2,1,0:T(1,128)S(1)} copy-done((f32[1,1,16,1,36864]{4,3,2,1,0:T(1,128)S(1)}, f32[1,1,16,1,36864]{4,3,2,1,0:T(1,128)}, u32[]{:S(2)}) %copy-start) | copy-done | bytes 2359320
  2.3 62.7 %panel_steps.1 = f32[16,288,128]{2,1,0:T(8,128)S(1)} custom-call(s32[1]{0:T(128)S(6)} %copy.5.panel_ref, f32[16,288,128]{2,1,0:T(8,128)S(1)} %bitcast.3), custom_call_target="tpu_custom_call" | custom-call | tf_op jit(solution)/shard_map/panel_steps/pallas_call | solution.py:517
  65.0 1.4 %copy.6 = f32[1,1,16,1,36864]{4,3,2,1,0:T(1,128)} copy(f32[1,1,16,1,36864]{4,3,2,1,0:T(1,128)S(1)} %bitcast.2) | data formatting | bytes 4718592
Async XLA Ops:
  0.7 1.7 %copy-start = (f32[1,1,16,1,36864]{4,3,2,1,0:T(1,128)S(1)}, f32[1,1,16,1,36864]{4,3,2,1,0:T(1,128)}, u32[]{:S(2)}) copy-start(f32[1,1,16,1,36864]{4,3,2,1,0:T(1,128)} %param.2) | copy-start | bytes 7077892

commit v8 on v7

--- a/solution.py
+++ b/solution.py
@@ -428,12 +428,13 @@
     live = [my_row > panel + t for t in range(3)]
     rest = (1, 2, 3)
     agenda = {
-        (0, 0): [lambda: other_core(1), lambda: other_core(2), row_start],
-        (0, 1): [lambda: side_ring(1, *rest), lambda: side_core(0, -1, 1)],
-        (0, 3): [lambda: main_ring(3), lambda: side_ring(3, 0)],
+        (0, 0): [lambda: other_core(1)],
+        (0, 1): [lambda: other_core(2), row_start, lambda: main_ring(2), lambda: side_ring(2, 0)],
+        (0, 3): [lambda: side_ring(1, *rest), lambda: side_core(0, -1, 1)],
+        (0, 5): [lambda: main_ring(3), lambda: side_ring(3, 0)],
         (1, 1): [lambda: side_ring(2, *rest), lambda: side_core(-2, 2)],
-        (1, 2): [lambda: main_ring(4), lambda: side_ring(4, 0)],
-        (1, 4): [lambda: main_core(0, -1, 1)],
+        (1, 3): [lambda: main_ring(4), lambda: side_ring(4, 0)],
+        (1, 5): [lambda: main_core(0, -1, 1)],
         (2, 2): [lambda: side_ring(3, *rest), lambda: side_core(-3, 3)],
         (2, 4): [lambda: main_core(-2, 2)],
     }
@@ -447,8 +448,6 @@
     main_ring(1)
     side_ring(1, 0)
     side_ring(0, *rest)
-    main_ring(2)
-    side_ring(2, 0)
     placed(0)
     app_tile(0, bt.at[0, 0])
     for t in range(3):

time: 66.5 us -> 66.5 us (level)
  no operation moved by 1% of the time
where the time goes in v8:
time: 66.5 us; the launch traced here: 66.4 us
  Pallas kernels  62.7 us (94%)
  local copies, waits for them, and re-layouts  3.07 us (5%)
  between operations  0.67 us (1%)
    pallas_call x1, Pallas kernels, body(): pl.pallas_call(kernel, out_shape=jax.ShapeDtypeStruct((16, 288, 128), F32...  62.7 us
    unnamed x3, local copies, waits for them, and re-layouts  3.07 us

profile of v8, /device:TPU:1, one launch (start us, length us, event | category | flops | bytes accessed | tf_op | source)
XLA Modules:
  0.0 66.4 jit_solution(602571561705036238)
XLA Ops:
  0.7 0.0 copy-start
  0.7 1.7 %copy-done = f32[1,1,16,1,36864]{4,3,2,1,0:T(1,128)S(1)} copy-done((f32[1,1,16,1,36864]{4,3,2,1,0:T(1,128)S(1)}, f32[1,1,16,1,36864]{4,3,2,1,0:T(1,128)}, u32[]{:S(2)}) %copy-start) | copy-done | bytes 2359320
  2.3 62.7 %panel_steps.1 = f32[16,288,128]{2,1,0:T(8,128)S(1)} custom-call(s32[1]{0:T(128)S(6)} %copy.5.panel_ref, f32[16,288,128]{2,1,0:T(8,128)S(1)} %bitcast.3), custom_call_target="tpu_custom_call" | custom-call | tf_op jit(solution)/shard_map/panel_steps/pallas_call | solution.py:516
  65.0 1.4 %copy.6 = f32[1,1,16,1,36864]{4,3,2,1,0:T(1,128)} copy(f32[1,1,16,1,36864]{4,3,2,1,0:T(1,128)S(1)} %bitcast.2) | data formatting | bytes 4718592
Async XLA Ops:
  0.7 1.7 %copy-start = (f32[1,1,16,1,36864]{4,3,2,1,0:T(1,128)S(1)}, f32[1,1,16,1,36864]{4,3,2,1,0:T(1,128)}, u32[]{:S(2)}) copy-start(f32[1,1,16,1,36864]{4,3,2,1,0:T(1,128)} %param.2) | copy-start | bytes 7077892
